TPU v7x, 256 devices: a whole 4x4x8 slice. The times are simulated.
256 devices in a mesh: ctx: 64 (over y, z, core), head: 4 (over x).
Axes of the slice: x: 4, y: 4, z: 8, core: 2. Of those that a mesh axis runs over, the one named last changes fastest.
Arguments:
- main_queries: bfloat16 [8192, 64, 576], P('ctx', 'head'), may hold values from -3.5 to 3.5
- latents: bfloat16 [8192, 576], P('ctx'), may hold values from -3.5 to 3.5
- main_lse: float32 [8192, 64], P('ctx', 'head'), may hold values from -20 to 40, as said below
- index_queries: bfloat16 [8192, 32, 128], P('ctx', 'head'), may hold values from -2 to 2
- index_keys: bfloat16 [8192, 128], P('ctx'), may hold values from -1.5 to 1.5
- index_weights: float32 [8192, 32], P('ctx', 'head'), may hold values from -3 to 3
Outputs:
- loss: float32 [], replicated
- index_query_grads: float32 [8192, 32, 128], P('ctx', 'head')
- index_weight_grads: float32 [8192, 32], P('ctx', 'head')
- index_key_grads: float32 [8192, 128], P(('ctx', 'head'))
Inputs may be any that keep to these rules, and one draw needn't show every extreme that they name: main_lse[t, h] is at least the logarithm of the sum over s <= t of exp(S[t, h, s]), so every term of masses is at most 1.
All inputs are finite; a program needn't handle non-finite values.
Results may differ from a plain program's by a relative error of at most 0.021.
Values may be sent and summed in bfloat16 or wider, within the bound.
No kernel may reach another device: no remote copies, remote signals or barrier semaphores. Data moves between devices by JAX's collectives and lax.ppermute only.
A program may use at most 128 MiB of HBM per device.

v0:
```python
import math

import jax
import jax.numpy as jnp
from jax import lax
from jax.sharding import PartitionSpec as P

score_scale = 192.0 ** (-0.5)
far_below = -1e30


def grouped(array, half_rows):
    return array.reshape((2, half_rows) + array.shape[1:])


def block_terms(queries, log_norms, index_rows, weights, row_pos, latent_rows, key_rows, key_pos):
    scores = (
        jnp.einsum("rhd,sd->rhs", queries, latent_rows, preferred_element_type=jnp.float32)
        * score_scale
    )
    visible = key_pos[None, :] <= row_pos[:, None]
    shifted = jnp.where(visible[:, None, :], scores - log_norms[:, :, None], far_below)
    masses = jnp.sum(jnp.exp(shifted), axis=1)
    raw_scores = jnp.einsum("rjd,sd->rjs", index_rows, key_rows, preferred_element_type=jnp.float32)
    logits = jnp.sum(weights[:, :, None] * jnp.maximum(raw_scores, 0.0), axis=1)
    return (masses, logits)


def first_pass(queries, log_norms, index_rows, weights, row_pos, latents, index_keys, all_tokens):
    row_count = queries.shape[1]
    initial = (
        jnp.zeros((2, row_count, all_tokens), jnp.float32),
        jnp.zeros((2, row_count, all_tokens), jnp.float32),
        jnp.zeros((all_tokens, index_keys.shape[1]), jnp.bfloat16),
    )
    latent_piece = lax.all_gather(latents, "ctx", axis=0, tiled=True)
    key_piece = lax.all_gather(index_keys, "ctx", axis=0, tiled=True)
    piece_rows = latent_piece.shape[0]
    key_span = math.gcd(piece_rows, 512)

    def step_block(step_index, current):
        masses, logits, kept_keys = current
        offset = step_index * key_span
        latent_rows = lax.dynamic_slice_in_dim(latent_piece, offset, key_span, 0)
        key_rows = lax.dynamic_slice_in_dim(key_piece, offset, key_span, 0)
        kept_keys = lax.dynamic_update_slice_in_dim(kept_keys, key_rows, offset, 0)
        key_pos = offset + jnp.arange(key_span, dtype=jnp.int32)
        for group_index in range(2):

            def step_compute(unused):
                return block_terms(
                    queries[group_index],
                    log_norms[group_index],
                    index_rows[group_index],
                    weights[group_index],
                    row_pos[group_index],
                    latent_rows,
                    key_rows,
                    key_pos,
                )

            def skip_block(unused):
                empty_block = jnp.zeros((row_count, key_span), jnp.float32)
                return (empty_block, empty_block)

            block_mass, block_logit = lax.cond(
                offset <= jnp.max(row_pos[group_index]), step_compute, skip_block, 0
            )
            where_at = (jnp.int32(group_index), jnp.int32(0), offset)
            masses = lax.dynamic_update_slice(masses, block_mass[None], where_at)
            logits = lax.dynamic_update_slice(logits, block_logit[None], where_at)
        return (masses, logits, kept_keys)

    return lax.fori_loop(0, piece_rows // key_span, step_block, initial)


def row_statistics(masses, logits, visible):
    target = masses / jnp.sum(masses, axis=2, keepdims=True)
    masked = jnp.where(visible, logits, far_below)
    row_top = jnp.max(masked, axis=2, keepdims=True)
    log_total = row_top[:, :, 0] + jnp.log(jnp.sum(jnp.exp(masked - row_top), axis=2))
    predicted = jnp.where(visible, jnp.exp(masked - log_total[:, :, None]), 0.0)
    coefficient = (predicted - target).astype(jnp.bfloat16)
    loss_part = jnp.sum(log_total) - jnp.sum(target * logits)
    return (coefficient, loss_part)


def second_pass(index_rows, weights, row_pos, coefficient, kept_keys, key_span):
    row_count = index_rows.shape[1]
    head_count = index_rows.shape[2]
    key_width = index_rows.shape[3]
    all_tokens = kept_keys.shape[0]
    initial = (
        jnp.zeros((2, row_count, head_count, key_width), jnp.float32),
        jnp.zeros((2, row_count, head_count), jnp.float32),
        jnp.zeros((all_tokens, key_width), jnp.float32),
    )

    def turn_step(step_index, carried):
        first_key = (step_index * key_span).astype(jnp.int32)
        key_rows = lax.dynamic_slice_in_dim(kept_keys, first_key, key_span, 0)
        for group_index in range(2):

            def turn_compute(current):
                query_grads, weight_grads, key_grads = current
                coeff_part = lax.dynamic_slice_in_dim(
                    coefficient[group_index], first_key, key_span, 1
                ).astype(jnp.float32)
                raw_scores = jnp.einsum(
                    "rjd,sd->rjs",
                    index_rows[group_index],
                    key_rows,
                    preferred_element_type=jnp.float32,
                )
                weight_add = jnp.sum(coeff_part[:, None, :] * jnp.maximum(raw_scores, 0.0), axis=2)
                gated = (
                    coeff_part[:, None, :]
                    * weights[group_index][:, :, None]
                    * jnp.where(raw_scores > 0.0, 1.0, 0.0)
                )
                mixed_terms = gated.astype(jnp.bfloat16)
                query_add = jnp.einsum(
                    "rjs,sd->rjd", mixed_terms, key_rows, preferred_element_type=jnp.float32
                )
                key_add = jnp.einsum(
                    "rjs,rjd->sd",
                    mixed_terms,
                    index_rows[group_index],
                    preferred_element_type=jnp.float32,
                )
                query_grads = query_grads.at[group_index].add(query_add)
                weight_grads = weight_grads.at[group_index].add(weight_add)
                old_keys = lax.dynamic_slice_in_dim(key_grads, first_key, key_span, 0)
                key_grads = lax.dynamic_update_slice_in_dim(
                    key_grads, old_keys + key_add, first_key, 0
                )
                return (query_grads, weight_grads, key_grads)

            def keep_state(current):
                return current

            carried = lax.cond(
                first_key <= jnp.max(row_pos[group_index]), turn_compute, keep_state, carried
            )
        return carried

    return lax.fori_loop(0, all_tokens // key_span, turn_step, initial)


def per_device(main_queries, latents, main_lse, index_queries, index_keys, index_weights):
    ctx_count = lax.axis_size("ctx")
    shard_rows = latents.shape[0]
    half_rows = shard_rows // 2
    all_tokens = shard_rows * ctx_count
    ctx_place = lax.axis_index("ctx")
    queries = grouped(main_queries, half_rows)
    log_norms = grouped(main_lse, half_rows)
    index_rows = grouped(index_queries, half_rows)
    weights = grouped(index_weights, half_rows)
    starts = jnp.stack([ctx_place * shard_rows, ctx_place * shard_rows + half_rows])
    row_pos = starts[:, None] + jnp.arange(half_rows, dtype=jnp.int32)[None, :]
    key_index = jnp.arange(all_tokens, dtype=jnp.int32)[None, None, :]
    masses, logits, kept_keys = first_pass(
        queries, log_norms, index_rows, weights, row_pos, latents, index_keys, all_tokens
    )
    masses, logits = (
        lax.psum_scatter(masses, "head", scatter_dimension=1, tiled=True),
        lax.psum_scatter(logits, "head", scatter_dimension=1, tiled=True),
    )
    share_rows = masses.shape[1]
    local_pos = lax.dynamic_slice_in_dim(
        row_pos, lax.axis_index("head") * share_rows, share_rows, 1
    )
    coefficient, loss_part = row_statistics(masses, logits, key_index <= local_pos[:, :, None])
    coefficient = lax.all_gather(coefficient, "head", axis=1, tiled=True)
    query_grads, weight_grads, key_grads = second_pass(
        index_rows, weights, row_pos, coefficient, kept_keys, 4 * shard_rows
    )
    loss = lax.psum(loss_part, ("ctx", "head")) / all_tokens
    key_grads = lax.psum_scatter(key_grads, ("ctx", "head"), scatter_dimension=0, tiled=True)
    query_grads = query_grads.reshape((shard_rows,) + query_grads.shape[2:])
    weight_grads = weight_grads.reshape((shard_rows,) + weight_grads.shape[2:])
    return (loss, query_grads, weight_grads, key_grads)


def solution(mesh):
    return jax.shard_map(
        per_device,
        mesh=mesh,
        in_specs=(
            P("ctx", "head", None),
            P("ctx", None),
            P("ctx", "head"),
            P("ctx", "head", None),
            P("ctx", None),
            P("ctx", "head"),
        ),
        out_specs=(P(), P("ctx", "head", None), P("ctx", "head"), P(("ctx", "head"), None)),
        check_vma=False,
    )
```

profile of v0, /device:TPU:2, one launch (start us, length us, event | category | flops | bytes accessed | tf_op | source)
XLA Modules:
  0.0 1933.2 jit_solution(16314122905337707013)
XLA Ops:
  9.5 4.9 copy.22
  15.3 75.8 %all-gather.6.cloned.1.call-done = bf16[8192,128]{1,0:T(8,128)(2,1)} async-done(((bf16[128,128]{1,0:T(8,128)(2,1)}), bf16[8192,128]{1,0:T(8,128)(2,1)}) %all-gather.6.cloned.1.call-update) | async-done | bytes 2097168 | tf_op jit(solution)/shard_map/all_gather | solution.py:37
  91.1 87.9 %all-gather.4.cloned.1.call-done = bf16[8192,576]{0,1:T(8,128)(2,1)} async-done(((bf16[128,576]{0,1:T(8,128)(2,1)}), bf16[8192,576]{0,1:T(8,128)(2,1)}) %all-gather.4.cloned.1.call-update) | async-done | bytes 9437200 | tf_op jit(solution)/shard_map/all_gather | solution.py:36
  179.0 2.5 broadcast.143
  181.5 2.4 broadcast.143.clone
  184.1 97.3 %while.43 = (s32[]{:T(128)}, f32[2,64,8192]{2,1,0:T(8,128)}, f32[2,64,8192]{2,1,0:T(8,128)}, bf16[8192,128]{1,0:T(8,128)(2,1)S(1)}, s32[]{:T(128)}, /*index=5*/b...) while((s32[]{:T(128)}, f32[2,64,8192]{2,1,0:T(8,128)}, ...), condition=%wide.region_11.12_spmd.clone, body=%wide.region_2.11_spmd.clone.sunk | while | flops 1347879552 | bytes 7709031 | solution.py:74
  185.1 1.1 constant_dynamic-slice_fusion.7
  186.9 3.4 conditional.12
  187.1 2.7 exponential_reduce_fusion
  191.7 3.4 conditional.13
  191.9 2.7 exponential_reduce_fusion.1
  197.5 1.1 constant_dynamic-slice_fusion.7
  203.2 1.1 constant_dynamic-slice_fusion.7
  214.5 1.1 constant_dynamic-slice_fusion.7
  220.2 1.1 constant_dynamic-slice_fusion.7
  237.1 1.1 constant_dynamic-slice_fusion.7
  265.4 1.1 constant_dynamic-slice_fusion.7
  271.1 1.1 constant_dynamic-slice_fusion.7
  282.8 146.0 %reduce-scatter.4.cloned.1.call-done = f32[2,16,8192]{2,1,0:T(8,128)} async-done(((f32[2,64,8192]{2,1,0:T(8,128)}), f32[2,16,8192]{2,1,0:T(8,128)}) %reduce-scatter.4.cloned.1.call-update) | async-done | bytes 1048592 | tf_op jit(solution)/shard_map/reduce_scatter | solution.py:168
  428.8 1.5 fusion.45
  430.3 50.2 %reduce-scatter.6.cloned.1.call-done = f32[2,16,8192]{2,1,0:T(8,128)} async-done(((f32[2,64,8192]{2,1,0:T(8,128)}), f32[2,16,8192]{2,1,0:T(8,128)}) %reduce-scatter.6.cloned.1.call-update) | async-done | bytes 1048592 | tf_op jit(solution)/shard_map/reduce_scatter | solution.py:167
  480.5 3.1 multiply_reduce_fusion.2
  484.2 1.1 subtract_convert_fusion
  485.4 33.5 %all-gather.8.cloned.1.call-done = bf16[2,64,8192]{2,1,0:T(8,128)(2,1)} async-done(((bf16[2,16,8192]{2,1,0:T(8,128)(2,1)}), bf16[2,64,8192]{2,1,0:T(8,128)(2,1)}) %all-gather.8.cloned.1.call-update) | async-done | bytes 2097168 | tf_op jit(solution)/shard_map/all_gather | solution.py:175
  519.0 2.2 broadcast_in_dim.112
  521.4 42.6 %while.42 = (s32[]{:T(128)}, f32[2,64,8,128]{3,2,1,0:T(8,128)S(1)}, f32[2,64,8]{2,1,0:T(8,128)S(1)}, f32[8192,128]{1,0:T(8,128)}, s32[]{:T(128)}, /*index=5*/s32...) while((s32[]{:T(128)}, f32[2,64,8,128]{3,2,1,0:T(8,128)S(1)}, ...), condition=%wide.region_27.28_spmd, body=%wide.region_20.27_spmd.sunk | while | flops 409796608 | bytes 15413759 | solution.py:147
  523.0 3.0 conditional.10
  523.5 2.1 fusion.21
  526.7 3.0 conditional.11
  527.2 2.1 fusion.33
  565.3 167.7 %psum.7 = f32[]{:T(128)} all-reduce(f32[]{:T(128)S(6)} %sub.44), channel_id=1, replica_groups=mesh['ctx'=64,'head'=4] {'ctx','head'}, use_global_device_ids=true, to_apply=%region_19.20 | all-reduce | flops 1 | bytes 8 | tf_op jit(solution)/shard_map/psum | solution.py:179
  734.3 1191.0 %reduce-scatter.8.cloned.1.call-done = f32[32,128]{1,0:T(8,128)} async-done(((f32[8192,128]{1,0:T(8,128)}), f32[32,128]{1,0:T(8,128)}) %reduce-scatter.8.cloned.1.call-update) | async-done | bytes 16400 | tf_op jit(solution)/shard_map/reduce_scatter | solution.py:180
  (297 shorter events, 85.2 us)
Async XLA Ops:
  7.2 7.3 copy-start.5
  7.2 83.9 %all-gather.6.cloned.1.call-start = ((), (), s32[]{:S(2)}) async-start(), calls=%async_computation.4 | async-start | bytes 2129920 | tf_op jit(solution)/shard_map/all_gather | solution.py:37
  7.9 171.0 %all-gather.4.cloned.1.call-start = ((), (), s32[]{:S(2)}) async-start(), calls=%async_computation.3 | async-start | bytes 9584640 | tf_op jit(solution)/shard_map/all_gather | solution.py:36
  8.7 420.1 %reduce-scatter.4.cloned.1.call-start = ((), (), s32[]{:S(2)}) async-start(), calls=%async_computation.5 | async-start | bytes 5242880 | tf_op jit(solution)/shard_map/reduce_scatter | solution.py:168
  181.5 2.7 copy-start.2
  281.4 1.3 copy-start.4
  281.5 199.1 %reduce-scatter.6.cloned.1.call-start = ((), (), s32[]{:S(2)}) async-start(), calls=%async_computation.6 | async-start | bytes 5242880 | tf_op jit(solution)/shard_map/reduce_scatter | solution.py:167
  282.8 236.2 %all-gather.8.cloned.1.call-start = ((), (), s32[]{:S(2)}) async-start(), calls=%async_computation.7 | async-start | bytes 2621440 | tf_op jit(solution)/shard_map/all_gather | solution.py:175
  430.3 53.9 %copy-start.3 = (f32[2,16,8192]{2,1,0:T(8,128)S(1)}, f32[2,16,8192]{2,1,0:T(8,128)}, u32[]{:S(2)}) copy-start(f32[2,16,8192]{2,1,0:T(8,128)} %reduce-scatter.4.cloned.1.call-done) | copy-start | bytes 3145732
  485.4 1439.9 %reduce-scatter.8.cloned.1.call-start = ((), (), s32[]{:S(2)}) async-start(), calls=%async_computation.8 | async-start | bytes 4210688 | tf_op jit(solution)/shard_map/reduce_scatter | solution.py:180
  519.0 2.4 copy-start
  564.0 1361.2 %copy-start.1 = (f32[2,64,8,128]{3,2,1,0:T(8,128)}, f32[2,64,8,128]{3,2,1,0:T(8,128)S(1)}, u32[]{:S(2)}) copy-start(f32[2,64,8,128]{3,2,1,0:T(8,128)S(1)} %get-tuple-element.646) | copy-start | bytes 1572868
Sparse Core Ops, SparseCore 0:
  10.8 80.2 all-gather.5
  93.6 85.2 all-gather.3
  281.6 147.1 reduce-scatter.3
  431.4 49.1 reduce-scatter.5
  485.5 33.3 all-gather.7
  564.2 1361.0 reduce-scatter.7
where the time goes:
time: 1940 us; the launch traced here: 1930 us
  waiting for transfers between devices  1590 us (82%)
  blocking collectives  168 us (9%)
  local copies, waits for them, and re-layouts  96.8 us (5%)
  loops' own time  44.4 us (2%)
    reduce_scatter x1, waiting for transfers between devices, per_device(): lax.psum_scatter(key_grads, ('ctx', 'head'), scatter_dimension=0, tiled=T...  1190 us
    psum x1, blocking collectives, per_device(): loss = lax.psum(loss_part, ('ctx', 'head')) / all_tokens  168 us
    reduce_scatter x1, waiting for transfers between devices, per_device(): lax.psum_scatter(logits, 'head', scatter_dimension=1, tiled=True)  146 us
    all_gather x1, waiting for transfers between devices, first_pass(): latent_piece = lax.all_gather(latents, 'ctx', axis=0, tiled=True)  87.9 us
    all_gather x1, waiting for transfers between devices, first_pass(): key_piece = lax.all_gather(index_keys, 'ctx', axis=0, tiled=True)  75.8 us
    reduce_scatter x1, waiting for transfers between devices, per_device(): lax.psum_scatter(masses, 'head', scatter_dimension=1, tiled=True)  50.2 us
  transfers between devices with their start and end apart: 6, of which 6 were waited for; matrix products, arithmetic and copies ran while one was open for 0% of the time, Pallas kernels for 0%

commit v1 on v0

v1 whole, which is shorter than its diff:
```python
import functools
import math

import jax
import jax.numpy as jnp
from jax import lax
from jax.experimental import pallas as pl
from jax.experimental.pallas import tpu as pltpu
from jax.sharding import PartitionSpec as P

f32, bf16 = jnp.float32, jnp.bfloat16
log2e = math.log2(math.e)
scale2 = 192.0 ** (-0.5) * log2e
far_below = -1e30

Y, Z, C, X = 4, 8, 2, 4
KB = 512
BLOCK = 128
PER = KB // BLOCK
LOSS_ROWS = 16


def ctx_groups(kind):
    place = lambda y, z, c: (y * Z + z) * C + c
    if kind == "y":
        return [[place(y, z, c) for y in range(Y)] for z in range(Z) for c in range(C)]
    return [[place(y, z, c) for z in range(Z)] for y in range(Y) for c in range(C)]


def wide(column, times):
    return jnp.concatenate([column] * times, axis=1)


def kernel(
    heads, iheads, starts, q_ref, lse_ref, iq_ref, iqt_ref, w_ref, keys_ref,
    qg_ref, wg_ref, kg_ref, masses, logits, coeffs,
):
    rows = masses.shape[1]
    latent = q_ref.shape[1]
    blocks = masses.shape[0]
    start = starts[0]
    slot = starts[1]
    count = (start + rows - 1) // KB + 1
    head_chunk = 16
    ihead_chunk = 16

    def key_block(kb, first, last):
        return jnp.concatenate([keys_ref[kb * PER + i, first:last, :] for i in range(PER)], axis=1)

    def first_step(kb, carried):
        lat = key_block(kb, 0, latent)
        total = jnp.zeros((rows, KB), f32)
        for part in range(heads // head_chunk):
            at = pl.ds(part * head_chunk * rows, head_chunk * rows)
            scores = jnp.dot(q_ref[at, :], lat, preferred_element_type=f32)
            mass = jnp.exp2(scores * scale2 - wide(lse_ref[at, :], PER))
            total = total + jnp.sum(mass.reshape(head_chunk, rows, KB), axis=0)
        key_pos = kb * KB + lax.broadcasted_iota(jnp.int32, (rows, KB), 1)
        row_pos = start + lax.broadcasted_iota(jnp.int32, (rows, KB), 0)
        visible = key_pos <= row_pos
        masses[kb] = jnp.where(visible, total, 0.0)
        keys = key_block(kb, latent, latent + BLOCK)
        logit = jnp.zeros((rows, KB), f32)
        for part in range(iheads // ihead_chunk):
            at = pl.ds(part * ihead_chunk * rows, ihead_chunk * rows)
            raw = jnp.dot(iq_ref[at, :], keys, preferred_element_type=f32)
            term = wide(w_ref[at, :], PER) * jnp.maximum(raw, 0.0)
            logit = logit + jnp.sum(term.reshape(ihead_chunk, rows, KB), axis=0)
        logits[kb] = jnp.where(visible, logit, far_below)
        return carried

    lax.fori_loop(0, count, first_step, 0)

    def sum_step(kb, carried):
        mass, top = carried
        return (mass + masses[kb], jnp.maximum(top, logits[kb]))

    mass, top = lax.fori_loop(
        0, count, sum_step, (jnp.zeros((rows, KB), f32), jnp.full((rows, KB), far_below, f32))
    )
    inverse = 1.0 / jnp.sum(mass, axis=1, keepdims=True)
    top = jnp.max(top, axis=1, keepdims=True)

    def exp_step(kb, carried):
        return carried + jnp.exp(logits[kb] - top)

    total = lax.fori_loop(0, count, exp_step, jnp.zeros((rows, KB), f32))
    log_total = top + jnp.log(jnp.sum(total, axis=1, keepdims=True))

    def coefficient_step(kb, carried):
        target = masses[kb] * inverse
        logit = logits[kb]
        coeffs[kb] = (jnp.exp(logit - log_total) - target).astype(bf16).astype(f32)
        return carried + target * logit

    cross = lax.fori_loop(0, count, coefficient_step, jnp.zeros((rows, KB), f32))
    loss = jnp.sum(log_total) - jnp.sum(cross)

    qg_ref[...] = jnp.zeros(qg_ref.shape, f32)
    wg_ref[...] = jnp.zeros(wg_ref.shape, f32)
    per_y = blocks * PER // (Y * C)

    def store_key_grads(kb, grads):
        for i in range(PER):
            pair = kb * (PER // 2) + i // 2
            at = pl.ds(pl.multiple_of((pair % per_y) * BLOCK, BLOCK), BLOCK)
            kg_ref[i % 2, pair // per_y, at, :] = grads[:, i * BLOCK : (i + 1) * BLOCK]

    def second_step(kb, carried):
        keys = key_block(kb, latent, latent + BLOCK)
        coefficient = coeffs[kb]
        key_grads = jnp.zeros((BLOCK, KB), f32)
        for part in range(iheads // ihead_chunk):
            at = pl.ds(part * ihead_chunk * rows, ihead_chunk * rows)
            raw = jnp.dot(iq_ref[at, :], keys, preferred_element_type=f32)
            raw = raw.reshape(ihead_chunk, rows, KB)
            weight = wide(w_ref[at, :], PER).reshape(ihead_chunk, rows, KB)
            add = (coefficient[None] * jnp.maximum(raw, 0.0)).reshape(ihead_chunk * rows, KB)
            add = sum(add[:, i * BLOCK : (i + 1) * BLOCK] for i in range(PER))
            wg_ref[at, :] += add
            mixed = jnp.where(raw > 0.0, coefficient[None] * weight, 0.0).astype(bf16)
            mixed = mixed.reshape(ihead_chunk * rows, KB)
            qg_ref[at, :] += lax.dot_general(
                mixed, keys, (((1,), (1,)), ((), ())), preferred_element_type=f32
            )
            key_grads = key_grads + jnp.dot(iqt_ref[:, at], mixed, preferred_element_type=f32)
        store_key_grads(kb, key_grads.astype(bf16))
        return carried

    lax.fori_loop(0, count, second_step, 0)

    def clear_step(kb, carried):
        store_key_grads(kb, jnp.zeros((BLOCK, KB), bf16))
        return carried

    lax.fori_loop(count, blocks, clear_step, 0)

    lane = lax.broadcasted_iota(jnp.int32, (LOSS_ROWS, BLOCK), 1)
    high = loss.astype(bf16).astype(f32)
    middle = (loss - high).astype(bf16).astype(f32)
    low = loss - high - middle
    piece = jnp.where(lane == slot * 3, high, 0.0)
    piece = piece + jnp.where(lane == slot * 3 + 1, middle, 0.0)
    piece = piece + jnp.where(lane == slot * 3 + 2, low, 0.0)
    for c in range(C):
        for y in range(Y):
            kg_ref[c, y, per_y * BLOCK :, :] = piece.astype(bf16)


def fused(start, slot, q, lse, iq, iqt, w, keys, rows, vmem=60 * 2**20):
    heads, iheads = q.shape[0] // rows, iq.shape[0] // rows
    tokens = keys.shape[0] * BLOCK
    blocks = tokens // KB
    per_y = tokens // BLOCK // (Y * C)
    vm = pl.BlockSpec(memory_space=pltpu.VMEM)
    return pl.pallas_call(
        functools.partial(kernel, heads, iheads),
        out_shape=(
            jax.ShapeDtypeStruct((iheads * rows, BLOCK), f32),
            jax.ShapeDtypeStruct((iheads * rows, BLOCK), f32),
            jax.ShapeDtypeStruct((C, Y, per_y * BLOCK + LOSS_ROWS, BLOCK), bf16),
        ),
        in_specs=[pl.BlockSpec(memory_space=pltpu.SMEM)] + [vm] * 6,
        out_specs=(vm, vm, vm),
        scratch_shapes=[pltpu.VMEM((blocks, rows, KB), f32)] * 3,
        compiler_params=pltpu.CompilerParams(vmem_limit_bytes=vmem),
        name="fused",
    )(jnp.stack([start, slot]).astype(jnp.int32), q, lse, iq, iqt, w, keys)


def head_exchange(array):
    return lax.all_to_all(array, "head", 0, 0, tiled=True)


def per_device(main_queries, latents, main_lse, index_queries, index_keys, index_weights):
    shard = latents.shape[0]
    ctx_count = lax.axis_size("ctx")
    all_tokens = shard * ctx_count
    ctx_place, head_place = lax.axis_index("ctx"), lax.axis_index("head")
    core = ctx_place % C
    y_place = ctx_place // (Z * C)
    rows = shard // X

    own = jnp.concatenate([latents, index_keys], axis=1).T
    keys = lax.all_gather(own[None], "ctx", axis=0, tiled=True)

    def by_rows(array):
        heads = array.shape[1]
        blocks = array.reshape((X, rows) + array.shape[1:])
        blocks = jnp.swapaxes(blocks, 1, 2).reshape((X * heads * rows,) + array.shape[2:])
        return head_exchange(blocks)

    q = by_rows(main_queries)
    lse = by_rows(main_lse) * log2e
    iq = by_rows(index_queries)
    w = by_rows(index_weights)
    lse = jnp.broadcast_to(lse[:, None], (lse.shape[0], BLOCK))
    w = jnp.broadcast_to(w[:, None], (w.shape[0], BLOCK))

    start = ctx_place * shard + head_place * rows
    qg, wg, kg = fused(start, y_place * C + core, q, lse, iq, iq.T, w, keys, rows)

    other = [(i, i ^ 1) for i in range(ctx_count)]
    sent = lax.dynamic_index_in_dim(kg, 1 - core, 0, keepdims=False)
    kept = lax.dynamic_index_in_dim(kg, core, 0, keepdims=False)
    came = lax.ppermute(sent, "ctx", other)
    part = (kept.astype(f32) + came.astype(f32)).astype(bf16)
    part = lax.all_to_all(part, "ctx", 0, 0, tiled=True, axis_index_groups=ctx_groups("y"))
    part = jnp.sum(part.astype(f32), axis=0)
    loss = jnp.broadcast_to(jnp.sum(part[Z * BLOCK, :]), (Z, 8, BLOCK))
    part = jnp.concatenate([part[: Z * BLOCK].reshape(Z, BLOCK, BLOCK), loss], axis=1)
    part = lax.all_to_all(part, "ctx", 0, 0, tiled=True, axis_index_groups=ctx_groups("z"))
    part = jnp.sum(part, axis=0)
    loss = jnp.broadcast_to(part[BLOCK:], (X, 8, BLOCK))
    part = jnp.concatenate([part[:BLOCK].T.reshape(X, rows, BLOCK), loss], axis=1)
    part = jnp.sum(head_exchange(part), axis=0)
    key_grads = part[:rows]
    loss = part[rows, 0] / all_tokens

    def by_heads(array):
        heads = array.shape[0] // rows // X
        back = head_exchange(array).reshape((X, heads, rows) + array.shape[1:])
        return jnp.swapaxes(back, 1, 2).reshape((shard, heads) + array.shape[1:])

    query_grads = by_heads(qg)
    weight_grads = by_heads(jnp.sum(wg, axis=1))
    return (loss, query_grads, weight_grads, key_grads)


def solution(mesh):
    return jax.shard_map(
        per_device,
        mesh=mesh,
        in_specs=(
            P("ctx", "head", None),
            P("ctx", None),
            P("ctx", "head"),
            P("ctx", "head", None),
            P("ctx", None),
            P("ctx", "head"),
        ),
        out_specs=(P(), P("ctx", "head", None), P("ctx", "head"), P(("ctx", "head"), None)),
        check_vma=False,
    )
```

time: 1940 us -> 245 us (0.13)
  waiting for transfers between devices: 1590 us -> 82.2 us
  blocking collectives: 168 us -> 28.3 us
  starting transfers between devices: 0.2 us -> 73.5 us
  local copies, waits for them, and re-layouts: 96.8 us -> 25.6 us
  loops' own time: 44.4 us -> 0 us
    reduce_scatter x3 -> x0, waiting for transfers between devices: 1390 us -> none  [the longest x1 1190 us: per_device(): lax.psum_scatter(key_grads, ('ctx', 'head'), scatter_dimension=0, tiled=T...]
    all_gather x3 -> x1, waiting for transfers between devices: 197 us -> 27.8 us  [per_device(): keys = lax.all_gather(own[None], 'ctx', axis=0, tiled=True)]
    psum x1 -> x0, blocking collectives: 168 us -> none  [per_device(): loss = lax.psum(loss_part, ('ctx', 'head')) / all_tokens]
    all_to_all x0 -> x8, starting transfers between devices: none -> 73.1 us  [the longest x1 38.7 us: per_device(): lax.all_to_all(part, 'ctx', 0, 0, tiled=True, axis_index_groups=ctx_group...]
    all_to_all x0 -> x8, waiting for transfers between devices: none -> 51.9 us  [the longest x7 37 us: head_exchange(): return lax.all_to_all(array, 'head', 0, 0, tiled=True)]
    dynamic_update_slice x64 -> x0, local copies, waits for them, and re-layouts: 48.7 us -> none  [the longest x32 22.7 us: step_block(): logits = lax.dynamic_update_slice(logits, block_logit[None], where_at)]
    another operation x66 -> x0, loops' own time: 44.4 us -> none  [the longest x1 21.5 us: second_pass(): return lax.fori_loop(0, all_tokens // key_span, turn_step, initial)]
    dynamic_slice x33 -> x0, local copies, waits for them, and re-layouts: 32.5 us -> none  [the longest x16 17.8 us: step_block(): latent_rows = lax.dynamic_slice_in_dim(latent_piece, offset, key_span, 0)]
  transfers between devices with their start and end apart: 6 -> 10, of which waited for: 6 -> 9; matrix products, arithmetic and copies ran while one was open for 0% -> 9% of each run, Pallas kernels for 0% -> 0%
where the time goes in v1:
time: 245 us; the launch traced here: 244 us
  waiting for transfers between devices  82.2 us (34%)
  starting transfers between devices  73.5 us (30%)
  blocking collectives  28.3 us (12%)
  local copies, waits for them, and re-layouts  25.6 us (10%)
  between operations  15.9 us (6%)
  Pallas kernels  11.2 us (5%)
  other arithmetic  7.11 us (3%)
    all_to_all x1, starting transfers between devices, per_device(): lax.all_to_all(part, 'ctx', 0, 0, tiled=True, axis_index_groups=ctx_group...  38.7 us
    all_to_all x7, waiting for transfers between devices, head_exchange(): return lax.all_to_all(array, 'head', 0, 0, tiled=True)  37 us
    all_to_all x7, starting transfers between devices, head_exchange(): return lax.all_to_all(array, 'head', 0, 0, tiled=True)  34.3 us
    all_to_all x1, blocking collectives, per_device(): lax.all_to_all(part, 'ctx', 0, 0, tiled=True, axis_index_groups=ctx_group...  28.3 us
    all_gather x1, waiting for transfers between devices, per_device(): keys = lax.all_gather(own[None], 'ctx', axis=0, tiled=True)  27.8 us
    all_to_all x1, waiting for transfers between devices, per_device(): lax.all_to_all(part, 'ctx', 0, 0, tiled=True, axis_index_groups=ctx_group...  14.9 us
    pallas_call x1, Pallas kernels, fused(): pl.pallas_call(functools.partial(kernel, heads, iheads), out_shape=(jax.S...  11.2 us
    all_to_all x5, local copies, waits for them, and re-layouts, head_exchange(): return lax.all_to_all(array, 'head', 0, 0, tiled=True)  7.31 us
  transfers between devices with their start and end apart: 10, of which 9 were waited for; matrix products, arithmetic and copies ran while one was open for 9% of the time, Pallas kernels for 0%

profile of v1, /device:TPU:2, one launch (start us, length us, event | category | flops | bytes accessed | tf_op | source)
XLA Modules:
  0.0 243.8 jit_solution(718668111525347699)
XLA Ops:
  7.2 0.9 copy.61
  8.1 1.6 maximum_bitcast_fusion
  11.2 5.5 %all-to-all-start.1 = ((f32[4,512,1]{1,2,0:T(1,128)}), f32[4,512,1]{1,2,0:T(1,128)S(1)}, u32[]{:S(2)}, u32[]{:S(2)}) async-start(f32[4,512,1]{1,2,0:T(1,128)} %all_to_all.64), calls=%async_computation.1 | async-start | bytes 16384 | tf_op jit(solution)/shard_map/all_to_all | solution.py:172
  16.7 1.7 copy.57
  18.4 2.2 all-to-all-done.1
  20.5 4.8 %all-to-all-start.2 = ((bf16[4,256,128]{2,1,0:T(8,128)(2,1)}), bf16[4,256,128]{2,1,0:T(8,128)(2,1)S(1)}, u32[]{:S(2)}, u32[]{:S(2)}) async-start(bf16[4,256,128]{2,1,0:T(8,128)(2,1)} %bitcast.10), calls=%async_computation.2 | async-start | bytes 524288 | tf_op jit(solution)/shard_map/all_to_all | solution.py:172
  25.4 5.0 %copy.51 = bf16[128,16,576]{2,1,0:T(8,128)(2,1)} copy(bf16[128,16,576]{0,2,1:T(8,128)(2,1)} %param.6) | data formatting | bytes 4718592 | tf_op args[0]
  30.3 2.3 copy.52
  32.6 2.6 %copy.53 = bf16[4,512,576]{1,2,0:T(8,128)(2,1)} copy(bf16[4,512,576]{2,1,0:T(8,128)(2,1)S(1)} %bitcast.49) | data formatting | bytes 4718592 | tf_op jit(solution)/shard_map/all_to_all | solution.py:172
  35.2 4.9 %all-to-all-start = ((bf16[4,512,576]{1,2,0:T(8,128)(2,1)}), bf16[4,512,576]{1,2,0:T(8,128)(2,1)S(1)}, u32[]{:S(2)}, u32[]{:S(2)}) async-start(bf16[4,512,576]{1,2,0:T(8,128)(2,1)} %copy.53), calls=%async_computation | async-start | bytes 4718592 | tf_op jit(solution)/shard_map/all_to_all | solution.py:172
  41.5 23.9 %all-to-all-done = bf16[4,512,576]{1,2,0:T(8,128)(2,1)S(1)} async-done(((bf16[4,512,576]{1,2,0:T(8,128)(2,1)}), bf16[4,512,576]{1,2,0:T(8,128)(2,1)S(1)}, u32[]{:S(2)}, u32[]{:S(2)}) %all-to-all-start) | async-done | bytes 2359328 | tf_op jit(solution)/shard_map/all_to_all | solution.py:172
  65.4 4.7 %all-to-all-start.3 = ((f32[4,256,1]{1,2,0:T(1,128)}), f32[4,256,1]{1,2,0:T(1,128)S(1)}, u32[]{:S(2)}, u32[]{:S(2)}) async-start(f32[4,256,1]{1,2,0:T(1,128)} %all_to_all.65), calls=%async_computation.3 | async-start | bytes 8192 | tf_op jit(solution)/shard_map/all_to_all | solution.py:172
  70.1 0.8 copy.67
  71.0 2.6 %copy.54 = bf16[4,512,576]{2,1,0:T(8,128)(2,1)} copy(bf16[4,512,576]{1,2,0:T(8,128)(2,1)S(1)} %all-to-all-done) | data formatting | bytes 4718592 | tf_op jit(solution)/shard_map/all_to_all | solution.py:172
  73.9 27.8 %all-gather.3.cloned.1.call-done = bf16[45056,128]{1,0:T(8,128)(2,1)} async-done(((bf16[704,128]{1,0:T(8,128)(2,1)}), bf16[45056,128]{1,0:T(8,128)(2,1)}) %all-gather.3.cloned.1.call-update) | async-done | bytes 11534352 | tf_op jit(solution)/shard_map/all_gather | solution.py:185
  101.7 1.3 broadcast_in_dim.10.lse_ref
  103.0 1.0 broadcast_in_dim.23.w_ref
  104.0 11.2 %fused.1 = (f32[1024,128]{1,0:T(8,128)}, f32[1024,128]{1,0:T(8,128)}, bf16[2,4,1040,128]{3,2,1,0:T(8,128)(2,1)}) custom-call(s32[2]{0:T(128)} %pad_add_fusion.starts, bf16[2048,576]{1,0:T(8,128)(2,1)} %bitcast.48, f32[2048,128]{1,0:T(8,128)} %broadcast_in_dim.10.lse_ref, bf16[1024,128]{1,0:T(8,128)(2,1)} %bitcast.52, bf16[128,1024]{1,0:T(8,128)(2,1)} %bitcast.55, ...), custom_call_target="tpu_custom_call" | custom-call | tf_op jit(solution)/shard_map/fused/pallas_call | solution.py:156
  115.2 1.4 dynamic-slice_bitcast_fusion
  117.0 2.6 %collective-permute-done = bf16[4,1040,128]{2,1,0:T(8,128)(2,1)} collective-permute-done((bf16[4,1040,128]{2,1,0:T(8,128)(2,1)S(1)}, bf16[4,1040,128]{2,1,0:T(8,128)(2,1)}, u32[]{:S(2)}, u32[]{:S(2)}) %collective-permute-start) | collective-permute-done | bytes 1064992 | tf_op jit(solution)/shard_map/ppermute | solution.py:206
  119.6 2.6 %fusion = bf16[4,1040,128]{2,1,0:T(8,128)(2,1)} fusion(bf16[4,1040,128]{2,1,0:T(8,128)(2,1)} %collective-permute-done, bf16[2,4,1040,128]{3,2,1,0:T(8,128)(2,1)S(1)} %copy-done.1, s32[]{:T(128)S(6)} %select_n.20), kind=kLoop, calls=%fused_computation.1 | loop fusion | flops 2129920 | bytes 3194884 | tf_op jit(solution)/shard_map/convert_element_type | solution.py:207
  122.2 38.7 %all-to-all-start.4 = ((bf16[4,1040,128]{2,1,0:T(8,128)(2,1)}), bf16[4,1040,128]{2,1,0:T(8,128)(2,1)S(1)}, u32[]{:S(2)}, u32[]{:S(2)}) async-start(bf16[4,1040,128]{2,1,0:T(8,128)(2,1)} %fusion), calls=%async_computation.4 | async-start | bytes 2129920 | tf_op jit(solution)/shard_map/all_to_all | solution.py:208
  160.9 0.8 reduce_sum.49
  161.7 14.9 %all-to-all-done.4 = bf16[4,1040,128]{2,1,0:T(8,128)(2,1)S(1)} async-done(((bf16[4,1040,128]{2,1,0:T(8,128)(2,1)}), bf16[4,1040,128]{2,1,0:T(8,128)(2,1)S(1)}, u32[]{:S(2)}, u32[]{:S(2)}) %all-to-all-start.4) | async-done | bytes 1064992 | tf_op jit(solution)/shard_map/all_to_all | solution.py:208
  176.6 4.8 %all-to-all-start.8 = ((f32[4,256,1]{1,2,0:T(1,128)}), f32[4,256,1]{1,2,0:T(1,128)S(1)}, u32[]{:S(2)}, u32[]{:S(2)}) async-start(f32[4,256,1]{1,2,0:T(1,128)} %bitcast.27), calls=%async_computation.8 | async-start | bytes 8192 | tf_op jit(solution)/shard_map/all_to_all | solution.py:172
  182.9 2.4 all-to-all-done.8
  185.2 28.3 %all_to_all.75 = f32[8,136,128]{2,1,0:T(8,128)S(1)} all-to-all(f32[8,136,128]{2,1,0:T(8,128)S(1)} %concatenate.10), channel_id=1, replica_groups={{0,8,16,24,32,40,48,56},{4,12,20,28,36,44,52,60},{64,72,80,88,96,104,11..., dimensions={0} | all-to-all | bytes 1114112 | tf_op jit(solution)/shard_map/all_to_all | solution.py:212
  213.6 4.9 %all-to-all-start.7 = ((f32[4,256,128]{2,1,0:T(8,128)}), f32[4,256,128]{2,1,0:T(8,128)S(1)}, u32[]{:S(2)}, u32[]{:S(2)}) async-start(f32[4,256,128]{2,1,0:T(8,128)} %bitcast.23), calls=%async_computation.7 | async-start | bytes 1048576 | tf_op jit(solution)/shard_map/all_to_all | solution.py:172
  219.3 5.8 %all-to-all-done.7 = f32[4,256,128]{2,1,0:T(8,128)S(1)} async-done(((f32[4,256,128]{2,1,0:T(8,128)}), f32[4,256,128]{2,1,0:T(8,128)S(1)}, u32[]{:S(2)}, u32[]{:S(2)}) %all-to-all-start.7) | async-done | bytes 524320 | tf_op jit(solution)/shard_map/all_to_all | solution.py:172
  225.1 4.7 %all-to-all-start.6 = ((f32[4,40,128]{2,1,0:T(8,128)}), f32[4,40,128]{2,1,0:T(8,128)S(1)}, u32[]{:S(2)}, u32[]{:S(2)}) async-start(f32[4,40,128]{2,1,0:T(8,128)} %pad_maximum_fusion), calls=%async_computation.6 | async-start | bytes 163840 | tf_op jit(solution)/shard_map/all_to_all | solution.py:172
  230.6 1.1 copy.64
  231.7 2.4 all-to-all-done.6
  (38 shorter events, 7.9 us)
Async XLA Ops:
  7.2 94.5 %all-gather.3.cloned.1.call-start = ((), (), s32[]{:S(2)}) async-start(), calls=%async_computation.9 | async-start | bytes 11714560 | tf_op jit(solution)/shard_map/all_gather | solution.py:185
  11.2 9.4 %all-to-all-start.1 = ((f32[4,512,1]{1,2,0:T(1,128)}), f32[4,512,1]{1,2,0:T(1,128)S(1)}, u32[]{:S(2)}, u32[]{:S(2)}) async-start(f32[4,512,1]{1,2,0:T(1,128)} %all_to_all.64), calls=%async_computation.1 | async-start | bytes 16384 | tf_op jit(solution)/shard_map/all_to_all | solution.py:172
  20.5 14.6 %all-to-all-start.2 = ((bf16[4,256,128]{2,1,0:T(8,128)(2,1)}), bf16[4,256,128]{2,1,0:T(8,128)(2,1)S(1)}, u32[]{:S(2)}, u32[]{:S(2)}) async-start(bf16[4,256,128]{2,1,0:T(8,128)(2,1)} %bitcast.10), calls=%async_computation.2 | async-start | bytes 524288 | tf_op jit(solution)/shard_map/all_to_all | solution.py:172
  35.2 4.9 %copy-start.3 = (f32[128,8]{0,1:T(8,128)S(1)}, f32[128,8]{0,1:T(8,128)}, u32[]{:S(2)}) copy-start(f32[128,8]{0,1:T(8,128)} %param.11) | copy-start | bytes 12292
  35.2 34.9 %copy-start = (bf16[4,256,128]{2,1,0:T(8,128)(2,1)}, bf16[4,256,128]{2,1,0:T(8,128)(2,1)S(1)}, u32[]{:S(2)}) copy-start(bf16[4,256,128]{2,1,0:T(8,128)(2,1)S(1)} %all-to-all-done.2) | copy-start | bytes 786436
  35.2 30.2 %all-to-all-start = ((bf16[4,512,576]{1,2,0:T(8,128)(2,1)}), bf16[4,512,576]{1,2,0:T(8,128)(2,1)S(1)}, u32[]{:S(2)}, u32[]{:S(2)}) async-start(bf16[4,512,576]{1,2,0:T(8,128)(2,1)} %copy.53), calls=%async_computation | async-start | bytes 4718592 | tf_op jit(solution)/shard_map/all_to_all | solution.py:172
  65.4 8.5 %all-to-all-start.3 = ((f32[4,256,1]{1,2,0:T(1,128)}), f32[4,256,1]{1,2,0:T(1,128)S(1)}, u32[]{:S(2)}, u32[]{:S(2)}) async-start(f32[4,256,1]{1,2,0:T(1,128)} %all_to_all.65), calls=%async_computation.3 | async-start | bytes 8192 | tf_op jit(solution)/shard_map/all_to_all | solution.py:172
  115.2 4.4 %copy-start.1 = (bf16[2,4,1040,128]{3,2,1,0:T(8,128)(2,1)S(1)}, bf16[2,4,1040,128]{3,2,1,0:T(8,128)(2,1)}, u32[]{:S(2)}) copy-start(bf16[2,4,1040,128]{3,2,1,0:T(8,128)(2,1)} %get-tuple-element.7) | copy-start | bytes 6389764
  116.7 2.9 %collective-permute-start = (bf16[4,1040,128]{2,1,0:T(8,128)(2,1)S(1)}, bf16[4,1040,128]{2,1,0:T(8,128)(2,1)}, u32[]{:S(2)}, u32[]{:S(2)}) collective-permute-start(bf16[4,1040,128]{2,1,0:T(8,128)(2,1)S(1)} %dynamic-slice_bitcast_fusion), channel_id=1, source_target_pairs={{0,4},{4,0},{8,12},{12,8},{16,20},{20,16},{24,28},{28,24},{32,36},... | collective-permute-start | bytes 3194888 | tf_op jit(solution)/shard_map/ppermute | solution.py:206
  119.6 41.3 %copy-start.2 = (f32[1024,128]{1,0:T(8,128)S(1)}, f32[1024,128]{1,0:T(8,128)}, u32[]{:S(2)}) copy-start(f32[1024,128]{1,0:T(8,128)} %get-tuple-element.9) | copy-start | bytes 1572868
  122.2 54.4 %all-to-all-start.4 = ((bf16[4,1040,128]{2,1,0:T(8,128)(2,1)}), bf16[4,1040,128]{2,1,0:T(8,128)(2,1)S(1)}, u32[]{:S(2)}, u32[]{:S(2)}) async-start(bf16[4,1040,128]{2,1,0:T(8,128)(2,1)} %fusion), calls=%async_computation.4 | async-start | bytes 2129920 | tf_op jit(solution)/shard_map/all_to_all | solution.py:208
  176.6 8.6 %all-to-all-start.8 = ((f32[4,256,1]{1,2,0:T(1,128)}), f32[4,256,1]{1,2,0:T(1,128)S(1)}, u32[]{:S(2)}, u32[]{:S(2)}) async-start(f32[4,256,1]{1,2,0:T(1,128)} %bitcast.27), calls=%async_computation.8 | async-start | bytes 8192 | tf_op jit(solution)/shard_map/all_to_all | solution.py:172
  213.6 11.5 %all-to-all-start.7 = ((f32[4,256,128]{2,1,0:T(8,128)}), f32[4,256,128]{2,1,0:T(8,128)S(1)}, u32[]{:S(2)}, u32[]{:S(2)}) async-start(f32[4,256,128]{2,1,0:T(8,128)} %bitcast.23), calls=%async_computation.7 | async-start | bytes 1048576 | tf_op jit(solution)/shard_map/all_to_all | solution.py:172
  225.1 9.0 %all-to-all-start.6 = ((f32[4,40,128]{2,1,0:T(8,128)}), f32[4,40,128]{2,1,0:T(8,128)S(1)}, u32[]{:S(2)}, u32[]{:S(2)}) async-start(f32[4,40,128]{2,1,0:T(8,128)} %pad_maximum_fusion), calls=%async_computation.6 | async-start | bytes 163840 | tf_op jit(solution)/shard_map/all_to_all | solution.py:172
Sparse Core Ops, SparseCore 0:
  10.7 90.9 all-gather.2

commit v2 on v1

v2 whole, which is shorter than its diff:
```python
import functools
import math

import jax
import jax.numpy as jnp
from jax import lax
from jax.experimental import pallas as pl
from jax.experimental.pallas import tpu as pltpu
from jax.sharding import Mesh
from jax.sharding import PartitionSpec as P

f32, bf16 = jnp.float32, jnp.bfloat16
log2e = math.log2(math.e)
scale2 = 192.0 ** (-0.5) * log2e
far_below = -1e30

Y, Z, C, X = 4, 8, 2, 4
BLOCK = 128
KB = 512
STEPS = Z * Y * C * BLOCK // KB
UNROLL = 4
GROUPS = 2
ROWS = 16
LOSS_ROWS = 16
HEAD_CHUNK = 32
IHEAD_CHUNK = 32


def wide(column):
    return jnp.concatenate([column] * (KB // BLOCK), axis=1)


def column_place(info, column):
    pair, second = column // 2, column % 2
    offset = jnp.where(second == 0, Z - pair, jnp.where(pair == 0, Z // 2, pair))
    return (info[2] + offset) % Z


def y_place(info, index):
    return (info[1] + index) % Y


def step_facts(info, step, group):
    pair, y = step // Y, y_place(info, step % Y)
    first = (y * Z + column_place(info, 2 * pair)) * (C * BLOCK)
    second = (y * Z + column_place(info, 2 * pair + 1)) * (C * BLOCK)
    start = jnp.where(group == 0, info[0], info[4])
    needed = jnp.minimum(first, second) < start + ROWS
    lane = lax.broadcasted_iota(jnp.int32, (ROWS, KB), 1)
    base = jnp.where(lane < C * BLOCK, first, second)
    core = jnp.where(lane % (C * BLOCK) < BLOCK, info[3], 1 - info[3])
    key_pos = base + core * BLOCK + lane % BLOCK
    row_pos = start + lax.broadcasted_iota(jnp.int32, (ROWS, KB), 0)
    return needed, key_pos <= row_pos


def step_block(cols, step, first, last):
    pair, y = step // Y, step % Y
    return jnp.concatenate(
        [cols[2 * pair + i, side, y, first:last, :] for i in range(2) for side in range(C)],
        axis=1,
    )


def score_step(info, step, group, block, q_ref, lse_ref, iq_ref, w_ref, masses, logits, tops):
    heads, _, latent = q_ref.shape[1:]
    iheads = iq_ref.shape[1] // ROWS
    needed, visible = step_facts(info, step, group)

    @pl.when(needed)
    def compute():
        lat = block(0, latent)
        total = jnp.zeros((ROWS, KB), f32)
        for part in range(heads // HEAD_CHUNK):
            at = pl.ds(part * HEAD_CHUNK * ROWS, HEAD_CHUNK * ROWS)
            queries = q_ref[group, pl.ds(part * HEAD_CHUNK, HEAD_CHUNK)]
            queries = queries.reshape(HEAD_CHUNK * ROWS, latent)
            scores = jnp.dot(queries, lat, preferred_element_type=f32)
            mass = jnp.exp2(scores * scale2 - wide(lse_ref[group, at, :]))
            total = total + jnp.sum(mass.reshape(HEAD_CHUNK, ROWS, KB), axis=0)
        masses[group, step] = jnp.where(visible, total, 0.0)
        keys = block(latent, latent + BLOCK)
        logit = jnp.zeros((ROWS, KB), f32)
        for part in range(iheads // IHEAD_CHUNK):
            at = pl.ds(part * IHEAD_CHUNK * ROWS, IHEAD_CHUNK * ROWS)
            raw = jnp.dot(iq_ref[group, at, :], keys, preferred_element_type=f32)
            term = wide(w_ref[group, at, :]) * jnp.maximum(raw, 0.0)
            logit = logit + jnp.sum(term.reshape(IHEAD_CHUNK, ROWS, KB), axis=0)
        logit = jnp.where(visible, logit, far_below)
        logits[group, step] = logit
        tops[group] = jnp.maximum(tops[group], logit)

    @pl.when(jnp.logical_not(needed))
    def skip():
        masses[group, step] = jnp.zeros((ROWS, KB), f32)
        logits[group, step] = jnp.full((ROWS, KB), far_below, f32)


def column_copies(column_refs, cols, sems):
    copies = []
    for column, pieces in enumerate(column_refs):
        group = []
        for side, part in enumerate(pieces):
            at = 0
            for i, piece in enumerate(part):
                size = piece.shape[0]
                group.append(
                    pltpu.make_async_copy(
                        piece, cols.at[column, side, pl.ds(at, size)], sems.at[column, side, i]
                    )
                )
                at += size
        copies.append(group)
    return copies


def kernel(info, lse_ref, iq_ref, w_ref, iqt_ref, *refs):
    query_refs, refs = refs[:GROUPS], refs[GROUPS:]
    column_refs = [((refs[2 * k],), (refs[2 * k + 1],)) for k in range(Z - 1)]
    far, refs = refs[2 * (Z - 1) : 2 * (Z - 1) + 4], refs[2 * (Z - 1) + 4 :]
    column_refs.insert(1, ((far[0], far[1]), (far[2], far[3])))
    rows_ref, kept_ref, sent_ref, q_all, masses, logits, tops, scales, key_grads, wg_ref = refs[:10]
    cols, sems, q_sems = refs[10:]
    latent = q_all.shape[-1]
    per = q_all.shape[1] // X
    iheads = iq_ref.shape[1] // ROWS
    copies = column_copies(column_refs, cols, sems)
    query_copies = [
        pltpu.make_async_copy(
            source.at[x, pl.ds(0, per)], q_all.at[group, pl.ds(x * per, per)], q_sems.at[group, x]
        )
        for group, source in enumerate(query_refs)
        for x in range(X)
    ]
    for copy in query_copies:
        copy.start()
    for group in copies:
        for copy in group:
            copy.start()
    own_rows = iheads // X * ROWS
    rows_ref[...] = jnp.zeros(rows_ref.shape, f32)
    wg_ref[...] = jnp.zeros(wg_ref.shape, f32)
    tops[...] = jnp.full(tops.shape, far_below, f32)
    for copy in query_copies:
        copy.wait()

    def first_step(step, carried):
        for pair in range(Z // 2):

            @pl.when(step == pair * Y)
            def arrive():
                for copy in copies[2 * pair] + copies[2 * pair + 1]:
                    copy.wait()

        block = functools.partial(step_block, cols, step)

        def one_group(group, carried):
            score_step(
                info, step, group, block, q_all, lse_ref, iq_ref, w_ref, masses, logits, tops
            )
            return carried

        return lax.fori_loop(0, GROUPS, one_group, carried)

    lax.fori_loop(0, STEPS, first_step, 0)

    loss = jnp.float32(0.0)
    for group in range(GROUPS):
        top = jnp.max(tops[group], axis=1, keepdims=True)

        def exp_step(kb, carried):
            mass_sum, exp_sum, cross = carried
            for i in range(UNROLL):
                at = kb * UNROLL + i
                mass, logit = masses[group, at], logits[group, at]
                power = jnp.exp(logit - top)
                logits[group, at] = power
                mass_sum = mass_sum + mass
                exp_sum = exp_sum + power
                cross = cross + mass * logit
            return mass_sum, exp_sum, cross

        none = jnp.zeros((ROWS, KB), f32)
        sums = lax.fori_loop(0, STEPS // UNROLL, exp_step, (none, none, none))
        mass_sum, exp_sum, cross = [jnp.sum(part, axis=1, keepdims=True) for part in sums]
        scales[group, 0] = jnp.broadcast_to(1.0 / mass_sum, (ROWS, BLOCK))
        scales[group, 1] = jnp.broadcast_to(1.0 / exp_sum, (ROWS, BLOCK))
        loss = loss + jnp.sum(top + jnp.log(exp_sum) - cross / mass_sum)

    def second_step(kb, carried):
        key_grads[...] = jnp.zeros((BLOCK, KB), f32)

        def one_group(group, carried):
            needed, _ = step_facts(info, kb, group)

            @pl.when(needed)
            def compute():
                keys = step_block(cols, kb, latent, latent + BLOCK)
                target = masses[group, kb] * wide(scales[group, 0])
                coefficient = logits[group, kb] * wide(scales[group, 1]) - target
                coefficient = coefficient.astype(bf16).astype(f32)
                for part in range(iheads // IHEAD_CHUNK):
                    at = pl.ds(part * IHEAD_CHUNK * ROWS, IHEAD_CHUNK * ROWS)
                    raw = jnp.dot(iq_ref[group, at, :], keys, preferred_element_type=f32)
                    raw = raw.reshape(IHEAD_CHUNK, ROWS, KB)
                    weight = wide(w_ref[group, at, :]).reshape(IHEAD_CHUNK, ROWS, KB)
                    add = coefficient[None] * jnp.maximum(raw, 0.0)
                    add = add.reshape(IHEAD_CHUNK * ROWS, KB)
                    add = sum(add[:, i * BLOCK : (i + 1) * BLOCK] for i in range(KB // BLOCK))
                    wg_ref[group, at, :] += add
                    mixed = jnp.where(raw > 0.0, coefficient[None] * weight, 0.0).astype(bf16)
                    mixed = mixed.reshape(IHEAD_CHUNK * ROWS, KB)
                    grads = lax.dot_general(
                        mixed, keys, (((1,), (1,)), ((), ())), preferred_element_type=f32
                    )
                    for i in range(IHEAD_CHUNK * ROWS // own_rows):
                        x = part * (IHEAD_CHUNK * ROWS // own_rows) + i
                        grad = grads[i * own_rows : (i + 1) * own_rows]
                        rows_ref[x, group, 0:own_rows, :] += grad
                    key_grads[...] += jnp.dot(
                        iqt_ref[group, :, at], mixed, preferred_element_type=f32
                    )

            return carried

        carried = lax.fori_loop(0, GROUPS, one_group, carried)
        for i in range(2):
            z = column_place(info, 2 * (kb // Y) + i)
            at = pl.ds(pl.multiple_of(z * BLOCK, BLOCK), BLOCK)
            for side, ref in enumerate((kept_ref, sent_ref)):
                lanes = (i * C + side) * BLOCK
                ref[kb % Y, at, :] = key_grads[:, lanes : lanes + BLOCK].astype(bf16)
        return carried

    lax.fori_loop(0, STEPS, second_step, 0)

    for x in range(X):
        for group in range(GROUPS):
            sums = jnp.sum(wg_ref[group, x * own_rows : (x + 1) * own_rows, :].T, axis=0)
            rows_ref[x, group, own_rows:, :] = jnp.broadcast_to(sums[None], (8, own_rows))

    lane = lax.broadcasted_iota(jnp.int32, (LOSS_ROWS, BLOCK), 1)
    slot = (info[1] * C + info[3]) * 3
    high = loss.astype(bf16).astype(f32)
    middle = (loss - high).astype(bf16).astype(f32)
    low = loss - high - middle
    piece = jnp.where(lane == slot, high, 0.0)
    piece = piece + jnp.where(lane == slot + 1, middle, 0.0)
    piece = piece + jnp.where(lane == slot + 2, low, 0.0)
    for ref in (kept_ref, sent_ref):
        for y in range(Y):
            ref[y, Z * BLOCK :, :] = piece.astype(bf16)


vmem_spec = pl.BlockSpec(memory_space=pltpu.VMEM)
smem_spec = pl.BlockSpec(memory_space=pltpu.SMEM)
any_spec = pl.BlockSpec(memory_space=pl.ANY)
vmem_limit = 56 * 2**20


def fused(info, lse, iq, w, queries, heads, columns, far):
    piece = columns[0][0]
    latent = queries[0].shape[-1]
    flat = [array for pair in columns for array in pair] + [a for pair in far for a in pair]
    return pl.pallas_call(
        kernel,
        out_shape=(
            jax.ShapeDtypeStruct((X, GROUPS, iq.shape[1] // X + 8, BLOCK), f32),
            jax.ShapeDtypeStruct((Y, Z * BLOCK + LOSS_ROWS, BLOCK), bf16),
            jax.ShapeDtypeStruct((Y, Z * BLOCK + LOSS_ROWS, BLOCK), bf16),
        ),
        in_specs=[smem_spec] + [vmem_spec] * 4 + [any_spec] * (len(flat) + GROUPS),
        out_specs=(vmem_spec,) * 3,
        scratch_shapes=[
            pltpu.VMEM((GROUPS, heads, ROWS, latent), bf16),
            pltpu.VMEM((GROUPS, STEPS, ROWS, KB), f32),
            pltpu.VMEM((GROUPS, STEPS, ROWS, KB), f32),
            pltpu.VMEM((GROUPS, ROWS, KB), f32),
            pltpu.VMEM((GROUPS, 2, ROWS, BLOCK), f32),
            pltpu.VMEM((BLOCK, KB), f32),
            pltpu.VMEM(iq.shape, f32),
            pltpu.VMEM((Z, C) + piece.shape, bf16),
            pltpu.SemaphoreType.DMA((Z, C, 2)),
            pltpu.SemaphoreType.DMA((GROUPS, X)),
        ],
        compiler_params=pltpu.CompilerParams(vmem_limit_bytes=vmem_limit),
        name="fused",
    )(info, lse, iq, w, jnp.swapaxes(iq, 1, 2), *queries, *flat)


def ring(axis, size, offset):
    return lambda array: lax.ppermute(
        array, axis, [(i, (i + offset) % size) for i in range(size)]
    )


def head_exchange(array):
    return lax.all_to_all(array, "head", 0, 0, tiled=True)


def terms(array):
    high = lax.reduce_precision(array, 8, 7)
    middle = lax.reduce_precision(array - high, 8, 7)
    low = array - high - middle
    return [part.astype(bf16) for part in (high, middle, low)]


def per_device(main_queries, latents, main_lse, index_queries, index_keys, index_weights):
    shard, heads, latent = main_queries.shape
    iheads = index_queries.shape[1]
    all_tokens = shard * Y * Z * C
    y, z, core, head = (lax.axis_index(name) for name in ("y", "z", "core", "head"))

    def first_token(y):
        return ((y * Z + z) * C + core) * shard

    start = first_token(y) + head * ROWS
    mirror_start = first_token(Y - 1 - y) + shard // 2 + head * ROWS
    info = jnp.stack([start, y, z, core, mirror_start]).astype(jnp.int32)
    up, down, swap = ring("z", Z, 1), ring("z", Z, -1), ring("core", C, 1)

    def mirror(array):
        return lax.ppermute(array, "y", [(i, Y - 1 - i) for i in range(Y)])

    extra = [index_queries.reshape(shard, -1)] + terms(main_lse) + terms(index_weights)
    used = sum(part.shape[1] for part in extra)
    more = -(-used // latent)
    extra.append(jnp.zeros((shard, more * latent - used), bf16))
    extra = jnp.concatenate(extra, axis=1).reshape(shard, more, latent)
    packed = jnp.concatenate([main_queries, extra], axis=1)
    packed = packed.reshape(GROUPS, X, ROWS, heads + more, latent)
    packed = jnp.swapaxes(packed, 2, 3)
    packed = (head_exchange(packed[0]), head_exchange(mirror(packed[1])))
    extra = jnp.stack([part[:, heads:] for part in packed])
    extra = jnp.swapaxes(extra, 2, 3).reshape(GROUPS, X, ROWS, more * latent)

    def column_of(first, count):
        part = extra[..., first : first + 3 * count].astype(f32)
        part = part.reshape(GROUPS, X, ROWS, 3, count)
        part = part[..., 0, :] + part[..., 1, :] + part[..., 2, :]
        part = jnp.swapaxes(part, 2, 3).reshape(GROUPS, -1, 1)
        return part

    size = iheads * BLOCK
    iq = extra[..., :size].reshape(GROUPS, X, ROWS, iheads, BLOCK)
    iq = jnp.swapaxes(iq, 2, 3).reshape(GROUPS, -1, BLOCK)
    lse = column_of(size, heads) * log2e
    w = column_of(size + 3 * heads, iheads)
    lse = jnp.broadcast_to(lse, lse.shape[:2] + (BLOCK,))
    w = jnp.broadcast_to(w, w.shape[:2] + (BLOCK,))

    own = jnp.concatenate([latents, index_keys], axis=1).T
    column = jnp.stack(
        [own, ring("y", Y, -1)(own), ring("y", Y, 2)(own), ring("y", Y, 1)(own)]
    )
    columns = [column]
    above = below = column
    for _ in range(Z // 2 - 1):
        below, above = up(below), down(above)
        columns += [below, above]
    far = (up(below[: Y // 2]), down(above[Y // 2 :]))
    pairs = [(array, swap(array)) for array in columns]
    far = (far, tuple(swap(array) for array in far))

    row_grads, kept, sent = fused(info, lse, iq, w, packed, heads * X, pairs, far)

    per = iheads * ROWS
    back = head_exchange(row_grads)
    mirrored = mirror(back[:, 1])
    query_grads = jnp.stack([back[:, 0, :per], mirrored[:, :per]])
    query_grads = query_grads.reshape(GROUPS, X, iheads, ROWS, BLOCK)
    query_grads = jnp.swapaxes(query_grads, 2, 3).reshape(shard, iheads, BLOCK)
    weight_grads = jnp.stack([back[:, 0, per], mirrored[:, per]])
    weight_grads = weight_grads.reshape(GROUPS, X, iheads, ROWS)
    weight_grads = jnp.swapaxes(weight_grads, 2, 3).reshape(shard, iheads)

    rows = shard // X
    came = swap(sent)
    parts = [(kept[i].astype(f32) + came[i].astype(f32)).astype(bf16) for i in range(Y)]
    parts = [parts[0]] + [ring("y", Y, i)(parts[i]) for i in range(1, Y)]
    part = sum(array.astype(f32) for array in parts)
    loss = jnp.sum(part[Z * BLOCK, :]) + 0.0 * back[0, 0, 0, 0]
    part = jnp.swapaxes(part[: Z * BLOCK].reshape(Z, BLOCK, BLOCK), 1, 2)
    part = part.reshape(Z * X, rows, BLOCK)
    loss = jnp.broadcast_to(loss, (Z * X, 8, BLOCK))
    part = jnp.concatenate([part, loss], axis=1)
    part = lax.all_to_all(part, ("z", "head"), 0, 0, tiled=True)
    part = jnp.sum(part, axis=0)
    key_grads = part[:rows]
    loss = part[rows, 0] / all_tokens
    return (loss, query_grads, weight_grads, key_grads)


def solution(mesh):
    places = Mesh(mesh.devices.reshape(Y, Z, C, X), ("y", "z", "core", "head"))
    ctx = ("y", "z", "core")
    return jax.shard_map(
        per_device,
        mesh=places,
        in_specs=(
            P(ctx, "head", None),
            P(ctx, None),
            P(ctx, "head"),
            P(ctx, "head", None),
            P(ctx, None),
            P(ctx, "head"),
        ),
        out_specs=(P(), P(ctx, "head", None), P(ctx, "head"), P(ctx + ("head",), None)),
        check_vma=False,
    )
```

time: 245 us -> 203 us (0.83)
  blocking collectives: 28.3 us -> 0 us
  Pallas kernels: 11.2 us -> 36.3 us
  starting transfers between devices: 73.5 us -> 61.2 us
  between operations: 15.9 us -> 4.07 us
  waiting for transfers between devices: 82.2 us -> 70.6 us
  local copies, waits for them, and re-layouts: 25.6 us -> 22.7 us
    ppermute x1 -> x26, waiting for transfers between devices: 2.55 us -> 50.3 us  [the longest x24 44 us: ring(): lax.ppermute(array, axis, [(i, (i + offset) % size) for i in range(size)])]
    ppermute x1 -> x26, starting transfers between devices: 0.35 us -> 31.1 us  [the longest x24 26.3 us: ring(): lax.ppermute(array, axis, [(i, (i + offset) % size) for i in range(size)])]
    all_to_all x1 -> x0, blocking collectives: 28.3 us -> none  [per_device(): lax.all_to_all(part, 'ctx', 0, 0, tiled=True, axis_index_groups=ctx_group...]
    all_gather x1 -> x0, waiting for transfers between devices: 27.8 us -> none  [per_device(): keys = lax.all_gather(own[None], 'ctx', axis=0, tiled=True)]
    all_to_all x7 -> x3, waiting for transfers between devices: 37 us -> 11.6 us  [head_exchange(): return lax.all_to_all(array, 'head', 0, 0, tiled=True)]
    pallas_call x1, Pallas kernels: 11.2 us -> 36.3 us  [fused(): pl.pallas_call(kernel, out_shape=(jax.ShapeDtypeStruct((X, GROUPS, iq.sha...]
    all_to_all x1, starting transfers between devices: 38.7 us -> 15.6 us  [per_device(): part = lax.all_to_all(part, ('z', 'head'), 0, 0, tiled=True)]
    all_to_all x7 -> x3, starting transfers between devices: 34.3 us -> 14.5 us  [head_exchange(): return lax.all_to_all(array, 'head', 0, 0, tiled=True)]
  transfers between devices with their start and end apart: 10 -> 30, of which waited for: 9 -> 16; matrix products, arithmetic and copies ran while one was open for 9% -> 10% of each run, Pallas kernels for 0% -> 0%
where the time goes in v2:
time: 203 us; the launch traced here: 202 us
  waiting for transfers between devices  70.6 us (35%)
  starting transfers between devices  61.2 us (30%)
  Pallas kernels  36.3 us (18%)
  local copies, waits for them, and re-layouts  22.7 us (11%)
  other arithmetic  6.95 us (3%)
  between operations  4.07 us (2%)
    ppermute x24, waiting for transfers between devices, ring(): lax.ppermute(array, axis, [(i, (i + offset) % size) for i in range(size)])  44 us
    pallas_call x1, Pallas kernels, fused(): pl.pallas_call(kernel, out_shape=(jax.ShapeDtypeStruct((X, GROUPS, iq.sha...  36.3 us
    ppermute x24, starting transfers between devices, ring(): lax.ppermute(array, axis, [(i, (i + offset) % size) for i in range(size)])  26.3 us
    all_to_all x1, starting transfers between devices, per_device(): part = lax.all_to_all(part, ('z', 'head'), 0, 0, tiled=True)  15.6 us
    all_to_all x3, starting transfers between devices, head_exchange(): return lax.all_to_all(array, 'head', 0, 0, tiled=True)  14.5 us
    all_to_all x3, waiting for transfers between devices, head_exchange(): return lax.all_to_all(array, 'head', 0, 0, tiled=True)  11.6 us
    all_to_all x1, waiting for transfers between devices, per_device(): part = lax.all_to_all(part, ('z', 'head'), 0, 0, tiled=True)  8.65 us
    ppermute x2, waiting for transfers between devices, mirror(): return lax.ppermute(array, 'y', [(i, Y - 1 - i) for i in range(Y)])  6.3 us
  transfers between devices with their start and end apart: 30, of which 16 were waited for; matrix products, arithmetic and copies ran while one was open for 10% of the time, Pallas kernels for 0%

profile of v2, /device:TPU:2, one launch (start us, length us, event | category | flops | bytes accessed | tf_op | source)
XLA Modules:
  0.0 201.8 jit_solution(13298204113692299893)
XLA Ops:
  2.5 3.3 %collective-permute-start.2 = (bf16[704,128]{1,0:T(8,128)(2,1)S(1)}, bf16[704,128]{1,0:T(8,128)(2,1)S(1)}, u32[]{:S(2)}, u32[]{:S(2)}) collective-permute-start(bf16[704,128]{1,0:T(8,128)(2,1)S(1)} %get-tuple-element.16), channel_id=1, source_target_pairs={{0,128},{64,192},{128,0},{192,64},{1,129},{65,193},{129,1},{193,65... | collective-permute-start | bytes 540680 | tf_op jit(solution)/shard_map/ppermute | solution.py:292
  11.5 3.9 %copy.37 = bf16[128,16,576]{2,1,0:T(8,128)(2,1)S(1)} copy(bf16[128,16,576]{0,2,1:T(8,128)(2,1)} %param.6) | data formatting | bytes 4718592 | tf_op args[0]
  16.4 1.1 pad_maximum_fusion.refs_2_
  17.5 5.9 %collective-permute-start.7 = (bf16[4,704,128]{2,1,0:T(8,128)(2,1)S(1)}, bf16[4,704,128]{2,1,0:T(8,128)(2,1)S(1)}, u32[]{:S(2)}, u32[]{:S(2)}) collective-permute-start(bf16[4,704,128]{2,1,0:T(8,128)(2,1)S(1)} %pad_maximum_fusion.refs_2_), channel_id=1, source_target_pairs={{0,56},{8,0},{16,8},{24,16},{32,24},{40,32},{48,40},{56,48},{1,57}... | collective-permute-start | bytes 2162696 | tf_op jit(solution)/shard_map/ppermute | solution.py:292
  23.5 1.9 slice_bitcast_fusion.1
  25.4 2.3 %collective-permute-start = (bf16[4,18,16,576]{3,2,1,0:T(8,128)(2,1)}, bf16[4,18,16,576]{3,2,1,0:T(8,128)(2,1)}, u32[]{:S(2)}, u32[]{:S(2)}) collective-permute-start(bf16[4,18,16,576]{3,2,1,0:T(8,128)(2,1)} %get-tuple-element.11), channel_id=1, source_target_pairs={{0,192},{64,128},{128,64},{192,0},{1,193},{65,129},{129,65},{193,1... | collective-permute-start | bytes 3981320 | tf_op jit(solution)/shard_map/ppermute | solution.py:323
  27.6 4.8 %all-to-all-start = ((bf16[4,18,16,576]{3,2,1,0:T(8,128)(2,1)}), bf16[4,18,16,576]{3,2,1,0:T(8,128)(2,1)S(1)}, u32[]{:S(2)}, u32[]{:S(2)}) async-start(bf16[4,18,16,576]{3,2,1,0:T(8,128)(2,1)} %get-tuple-element.10), calls=%async_computation | async-start | bytes 2949120 | tf_op jit(solution)/shard_map/all_to_all | solution.py:298
  32.5 5.6 %collective-permute-done.7.refs_6_ = bf16[4,704,128]{2,1,0:T(8,128)(2,1)S(1)} collective-permute-done((bf16[4,704,128]{2,1,0:T(8,128)(2,1)S(1)}, bf16[4,704,128]{2,1,0:T(8,128)(2,1)S(1)}, u32[]{:S(2)}, u32[]{:S(2)}) %collective-permute-start.7) | collective-permute-done | bytes 720928 | tf_op jit(solution)/shard_map/ppermute | solution.py:292
  38.0 3.7 %collective-permute-start.11 = (bf16[4,704,128]{2,1,0:T(8,128)(2,1)S(1)}, bf16[4,704,128]{2,1,0:T(8,128)(2,1)}, u32[]{:S(2)}, u32[]{:S(2)}) collective-permute-start(bf16[4,704,128]{2,1,0:T(8,128)(2,1)S(1)} %collective-permute-done.7.refs_6_), channel_id=1, source_target_pairs={{0,56},{8,0},{16,8},{24,16},{32,24},{40,32},{48,40},{56,48},{1,57}... | collective-permute-start | bytes 2162696 | tf_op jit(solution)/shard_map/ppermute | solution.py:292
  41.7 8.0 %collective-permute-done.5.refs_4_ = bf16[4,704,128]{2,1,0:T(8,128)(2,1)} collective-permute-done((bf16[4,704,128]{2,1,0:T(8,128)(2,1)S(1)}, bf16[4,704,128]{2,1,0:T(8,128)(2,1)}, u32[]{:S(2)}, u32[]{:S(2)}) %collective-permute-start.5) | collective-permute-done | bytes 720928 | tf_op jit(solution)/shard_map/ppermute | solution.py:292
  49.7 5.8 %collective-permute-done.11.refs_10_ = bf16[4,704,128]{2,1,0:T(8,128)(2,1)} collective-permute-done((bf16[4,704,128]{2,1,0:T(8,128)(2,1)S(1)}, bf16[4,704,128]{2,1,0:T(8,128)(2,1)}, u32[]{:S(2)}, u32[]{:S(2)}) %collective-permute-start.11) | collective-permute-done | bytes 720928 | tf_op jit(solution)/shard_map/ppermute | solution.py:292
  55.4 3.8 %collective-permute-start.15 = (bf16[4,704,128]{2,1,0:T(8,128)(2,1)}, bf16[4,704,128]{2,1,0:T(8,128)(2,1)}, u32[]{:S(2)}, u32[]{:S(2)}) collective-permute-start(bf16[4,704,128]{2,1,0:T(8,128)(2,1)} %collective-permute-done.11.refs_10_), channel_id=1, source_target_pairs={{0,56},{8,0},{16,8},{24,16},{32,24},{40,32},{48,40},{56,48},{1,57}... | collective-permute-start | bytes 2162696 | tf_op jit(solution)/shard_map/ppermute | solution.py:292
  59.8 4.8 %all-to-all-start.1 = ((bf16[4,18,16,576]{3,2,1,0:T(8,128)(2,1)}), bf16[4,18,16,576]{3,2,1,0:T(8,128)(2,1)S(1)}, u32[]{:S(2)}, u32[]{:S(2)}) async-start(bf16[4,18,16,576]{3,2,1,0:T(8,128)(2,1)} %collective-permute-done), calls=%async_computation.1 | async-start | bytes 2949120 | tf_op jit(solution)/shard_map/all_to_all | solution.py:298
  64.6 1.6 collective-permute-done.9.refs_8_
  66.7 5.6 %collective-permute-done.15.refs_14_ = bf16[4,704,128]{2,1,0:T(8,128)(2,1)} collective-permute-done((bf16[4,704,128]{2,1,0:T(8,128)(2,1)}, bf16[4,704,128]{2,1,0:T(8,128)(2,1)}, u32[]{:S(2)}, u32[]{:S(2)}) %collective-permute-start.15) | collective-permute-done | bytes 720928 | tf_op jit(solution)/shard_map/ppermute | solution.py:292
  73.1 7.7 %all-to-all-done.1.refs_1_ = bf16[4,18,16,576]{3,2,1,0:T(8,128)(2,1)S(1)} async-done(((bf16[4,18,16,576]{3,2,1,0:T(8,128)(2,1)}), bf16[4,18,16,576]{3,2,1,0:T(8,128)(2,1)S(1)}, u32[]{:S(2)}, u32[]{:S(2)}) %all-to-all-start.1) | async-done | bytes 1327136 | tf_op jit(solution)/shard_map/all_to_all | solution.py:298
  81.4 1.8 slice.146
  83.1 1.7 slice.145
  87.9 8.2 %collective-permute-done.18.refs_17_ = bf16[2,704,128]{2,1,0:T(8,128)(2,1)} collective-permute-done((bf16[2,704,128]{2,1,0:T(8,128)(2,1)}, bf16[2,704,128]{2,1,0:T(8,128)(2,1)}, u32[]{:S(2)}, u32[]{:S(2)}) %collective-permute-start.18) | collective-permute-done | bytes 360480 | tf_op jit(solution)/shard_map/ppermute | solution.py:292
  96.0 1.9 collective-permute-done.17.refs_16_
  101.0 1.3 broadcast_in_dim.17.lse_ref
  102.4 36.3 %fused.1 = (f32[4,2,136,128]{3,2,1,0:T(8,128)}, bf16[4,1040,128]{2,1,0:T(8,128)(2,1)}, bf16[4,1040,128]{2,1,0:T(8,128)(2,1)}) custom-call(s32[5]{0:T(128)} %stack.62.info, f32[2,1024,128]{2,1,0:T(8,128)} %broadcast_in_dim.17.lse_ref, bf16[2,512,128]{2,1,0:T(8,128)(2,1)} %bitcast.83, f32[2,512,128]{2,1,0:T(8,128)} %broadcast_in_dim.19.w_ref, ...), custom_call_target="tpu_custom_call" | custom-call | tf_op jit(solution)/shard_map/fused/pallas_call | solution.py:265
  139.1 4.9 %all-to-all-start.2 = ((f32[4,2,136,128]{3,2,1,0:T(8,128)}), f32[4,2,136,128]{3,2,1,0:T(8,128)S(1)}, u32[]{:S(2)}, u32[]{:S(2)}) async-start(f32[4,2,136,128]{3,2,1,0:T(8,128)} %get-tuple-element.9), calls=%async_computation.2 | async-start | bytes 1114112 | tf_op jit(solution)/shard_map/all_to_all | solution.py:298
  145.0 3.2 %collective-permute-start.24 = (bf16[1040,128]{1,0:T(8,128)(2,1)}, bf16[1040,128]{1,0:T(8,128)(2,1)S(1)}, u32[]{:S(2)}, u32[]{:S(2)}) collective-permute-start(bf16[1040,128]{1,0:T(8,128)(2,1)} %get-tuple-element.13), channel_id=1, source_target_pairs={{0,192},{64,0},{128,64},{192,128},{1,193},{65,1},{129,65},{193,129... | collective-permute-start | bytes 798728 | tf_op jit(solution)/shard_map/ppermute | solution.py:292
  149.1 3.9 %all-to-all-done.2 = f32[4,2,136,128]{3,2,1,0:T(8,128)S(1)} async-done(((f32[4,2,136,128]{3,2,1,0:T(8,128)}), f32[4,2,136,128]{3,2,1,0:T(8,128)S(1)}, u32[]{:S(2)}, u32[]{:S(2)}) %all-to-all-start.2) | async-done | bytes 557088 | tf_op jit(solution)/shard_map/all_to_all | solution.py:298
  155.3 4.5 %collective-permute-done.24 = bf16[1040,128]{1,0:T(8,128)(2,1)S(1)} collective-permute-done((bf16[1040,128]{1,0:T(8,128)(2,1)}, bf16[1040,128]{1,0:T(8,128)(2,1)S(1)}, u32[]{:S(2)}, u32[]{:S(2)}) %collective-permute-start.24) | collective-permute-done | bytes 266272 | tf_op jit(solution)/shard_map/ppermute | solution.py:292
  159.7 1.2 collective-permute-done.23
  160.9 1.1 fusion.1
  164.4 15.6 %all-to-all-start.3 = ((f32[32,40,128]{2,1,0:T(8,128)}), f32[32,40,128]{2,1,0:T(8,128)S(1)}, u32[]{:S(2)}, u32[]{:S(2)}) async-start(f32[32,40,128]{2,1,0:T(8,128)} %concatenate.24), calls=%async_computation.3 | async-start | bytes 1310720 | tf_op jit(solution)/shard_map/all_to_all | solution.py:387
  180.0 2.5 %collective-permute-start.25 = (f32[4,136,128]{2,1,0:T(8,128)S(1)}, f32[4,136,128]{2,1,0:T(8,128)S(1)}, u32[]{:S(2)}, u32[]{:S(2)}) collective-permute-start(f32[4,136,128]{2,1,0:T(8,128)S(1)} %slice_bitcast_fusion.2), channel_id=1, source_target_pairs={{0,192},{64,128},{128,64},{192,0},{1,193},{65,129},{129,65},{193,1... | collective-permute-start | bytes 835592 | tf_op jit(solution)/shard_map/ppermute | solution.py:323
  182.6 5.8 %collective-permute-done.25 = f32[4,136,128]{2,1,0:T(8,128)S(1)} collective-permute-done((f32[4,136,128]{2,1,0:T(8,128)S(1)}, f32[4,136,128]{2,1,0:T(8,128)S(1)}, u32[]{:S(2)}, u32[]{:S(2)}) %collective-permute-start.25) | collective-permute-done | bytes 278560 | tf_op jit(solution)/shard_map/ppermute | solution.py:323
  190.2 8.6 %all-to-all-done.3 = f32[32,40,128]{2,1,0:T(8,128)S(1)} async-done(((f32[32,40,128]{2,1,0:T(8,128)}), f32[32,40,128]{2,1,0:T(8,128)S(1)}, u32[]{:S(2)}, u32[]{:S(2)}) %all-to-all-start.3) | async-done | bytes 655392 | tf_op jit(solution)/shard_map/all_to_all | solution.py:387
  (112 shorter events, 25.4 us)
Async XLA Ops:
  2.5 13.9 %collective-permute-start.2 = (bf16[704,128]{1,0:T(8,128)(2,1)S(1)}, bf16[704,128]{1,0:T(8,128)(2,1)S(1)}, u32[]{:S(2)}, u32[]{:S(2)}) collective-permute-start(bf16[704,128]{1,0:T(8,128)(2,1)S(1)} %get-tuple-element.16), channel_id=1, source_target_pairs={{0,128},{64,192},{128,0},{192,64},{1,129},{65,193},{129,1},{193,65... | collective-permute-start | bytes 540680 | tf_op jit(solution)/shard_map/ppermute | solution.py:292
  5.7 10.7 %collective-permute-start.1 = (bf16[704,128]{1,0:T(8,128)(2,1)S(1)}, bf16[704,128]{1,0:T(8,128)(2,1)}, u32[]{:S(2)}, u32[]{:S(2)}) collective-permute-start(bf16[704,128]{1,0:T(8,128)(2,1)S(1)} %get-tuple-element.16), channel_id=1, source_target_pairs={{0,192},{64,0},{128,64},{192,128},{1,193},{65,1},{129,65},{193,129... | collective-permute-start | bytes 540680 | tf_op jit(solution)/shard_map/ppermute | solution.py:292
  6.8 9.6 %collective-permute-start.3 = (bf16[704,128]{1,0:T(8,128)(2,1)S(1)}, bf16[704,128]{1,0:T(8,128)(2,1)}, u32[]{:S(2)}, u32[]{:S(2)}) collective-permute-start(bf16[704,128]{1,0:T(8,128)(2,1)S(1)} %get-tuple-element.16), channel_id=1, source_target_pairs={{0,64},{64,128},{128,192},{192,0},{1,65},{65,129},{129,193},{193,1... | collective-permute-start | bytes 540680 | tf_op jit(solution)/shard_map/ppermute | solution.py:292
  17.5 14.9 %copy-start.2 = (bf16[4,704,128]{2,1,0:T(8,128)(2,1)}, bf16[4,704,128]{2,1,0:T(8,128)(2,1)S(1)}, u32[]{:S(2)}) copy-start(bf16[4,704,128]{2,1,0:T(8,128)(2,1)S(1)} %pad_maximum_fusion.refs_2_) | copy-start | bytes 2162692
  17.5 20.5 %collective-permute-start.7 = (bf16[4,704,128]{2,1,0:T(8,128)(2,1)S(1)}, bf16[4,704,128]{2,1,0:T(8,128)(2,1)S(1)}, u32[]{:S(2)}, u32[]{:S(2)}) collective-permute-start(bf16[4,704,128]{2,1,0:T(8,128)(2,1)S(1)} %pad_maximum_fusion.refs_2_), channel_id=1, source_target_pairs={{0,56},{8,0},{16,8},{24,16},{32,24},{40,32},{48,40},{56,48},{1,57}... | collective-permute-start | bytes 2162696 | tf_op jit(solution)/shard_map/ppermute | solution.py:292
  25.4 34.4 %collective-permute-start = (bf16[4,18,16,576]{3,2,1,0:T(8,128)(2,1)}, bf16[4,18,16,576]{3,2,1,0:T(8,128)(2,1)}, u32[]{:S(2)}, u32[]{:S(2)}) collective-permute-start(bf16[4,18,16,576]{3,2,1,0:T(8,128)(2,1)} %get-tuple-element.11), channel_id=1, source_target_pairs={{0,192},{64,128},{128,64},{192,0},{1,193},{65,129},{129,65},{193,1... | collective-permute-start | bytes 3981320 | tf_op jit(solution)/shard_map/ppermute | solution.py:323
  27.6 31.6 %all-to-all-start = ((bf16[4,18,16,576]{3,2,1,0:T(8,128)(2,1)}), bf16[4,18,16,576]{3,2,1,0:T(8,128)(2,1)S(1)}, u32[]{:S(2)}, u32[]{:S(2)}) async-start(bf16[4,18,16,576]{3,2,1,0:T(8,128)(2,1)} %get-tuple-element.10), calls=%async_computation | async-start | bytes 2949120 | tf_op jit(solution)/shard_map/all_to_all | solution.py:298
  32.5 17.2 %collective-permute-start.5 = (bf16[4,704,128]{2,1,0:T(8,128)(2,1)S(1)}, bf16[4,704,128]{2,1,0:T(8,128)(2,1)}, u32[]{:S(2)}, u32[]{:S(2)}) collective-permute-start(bf16[4,704,128]{2,1,0:T(8,128)(2,1)S(1)} %pad_maximum_fusion.refs_2_), channel_id=1, source_target_pairs={{0,8},{8,16},{16,24},{24,32},{32,40},{40,48},{48,56},{56,0},{1,9},... | collective-permute-start | bytes 2162696 | tf_op jit(solution)/shard_map/ppermute | solution.py:292
  38.0 21.8 %copy-start.5 = (bf16[4,704,128]{2,1,0:T(8,128)(2,1)}, bf16[4,704,128]{2,1,0:T(8,128)(2,1)S(1)}, u32[]{:S(2)}) copy-start(bf16[4,704,128]{2,1,0:T(8,128)(2,1)S(1)} %collective-permute-done.7.refs_6_) | copy-start | bytes 2162692
  38.0 17.4 %collective-permute-start.11 = (bf16[4,704,128]{2,1,0:T(8,128)(2,1)S(1)}, bf16[4,704,128]{2,1,0:T(8,128)(2,1)}, u32[]{:S(2)}, u32[]{:S(2)}) collective-permute-start(bf16[4,704,128]{2,1,0:T(8,128)(2,1)S(1)} %collective-permute-done.7.refs_6_), channel_id=1, source_target_pairs={{0,56},{8,0},{16,8},{24,16},{32,24},{40,32},{48,40},{56,48},{1,57}... | collective-permute-start | bytes 2162696 | tf_op jit(solution)/shard_map/ppermute | solution.py:292
  49.7 16.5 %collective-permute-start.9 = (bf16[4,704,128]{2,1,0:T(8,128)(2,1)}, bf16[4,704,128]{2,1,0:T(8,128)(2,1)}, u32[]{:S(2)}, u32[]{:S(2)}) collective-permute-start(bf16[4,704,128]{2,1,0:T(8,128)(2,1)} %collective-permute-done.5.refs_4_), channel_id=1, source_target_pairs={{0,8},{8,16},{16,24},{24,32},{32,40},{40,48},{48,56},{56,0},{1,9},... | collective-permute-start | bytes 2162696 | tf_op jit(solution)/shard_map/ppermute | solution.py:292
  55.4 16.9 %collective-permute-start.15 = (bf16[4,704,128]{2,1,0:T(8,128)(2,1)}, bf16[4,704,128]{2,1,0:T(8,128)(2,1)}, u32[]{:S(2)}, u32[]{:S(2)}) collective-permute-start(bf16[4,704,128]{2,1,0:T(8,128)(2,1)} %collective-permute-done.11.refs_10_), channel_id=1, source_target_pairs={{0,56},{8,0},{16,8},{24,16},{32,24},{40,32},{48,40},{56,48},{1,57}... | collective-permute-start | bytes 2162696 | tf_op jit(solution)/shard_map/ppermute | solution.py:292
  59.8 21.0 %all-to-all-start.1 = ((bf16[4,18,16,576]{3,2,1,0:T(8,128)(2,1)}), bf16[4,18,16,576]{3,2,1,0:T(8,128)(2,1)S(1)}, u32[]{:S(2)}, u32[]{:S(2)}) async-start(bf16[4,18,16,576]{3,2,1,0:T(8,128)(2,1)} %collective-permute-done), calls=%async_computation.1 | async-start | bytes 2949120 | tf_op jit(solution)/shard_map/all_to_all | solution.py:298
  66.2 16.9 %collective-permute-start.13 = (bf16[4,704,128]{2,1,0:T(8,128)(2,1)}, bf16[4,704,128]{2,1,0:T(8,128)(2,1)}, u32[]{:S(2)}, u32[]{:S(2)}) collective-permute-start(bf16[4,704,128]{2,1,0:T(8,128)(2,1)} %collective-permute-done.9.refs_8_), channel_id=1, source_target_pairs={{0,8},{8,16},{16,24},{24,32},{32,40},{40,48},{48,56},{56,0},{1,9},... | collective-permute-start | bytes 2162696 | tf_op jit(solution)/shard_map/ppermute | solution.py:292
  66.2 18.7 %collective-permute-start.4 = (bf16[4,704,128]{2,1,0:T(8,128)(2,1)}, bf16[4,704,128]{2,1,0:T(8,128)(2,1)}, u32[]{:S(2)}, u32[]{:S(2)}) collective-permute-start(bf16[4,704,128]{2,1,0:T(8,128)(2,1)} %copy-done.2), channel_id=1, source_target_pairs={{0,4},{4,0},{1,5},{5,1},{2,6},{6,2},{3,7},{7,3},{8,12},{12,8},{9,1... | collective-permute-start | bytes 2162696 | tf_op jit(solution)/shard_map/ppermute | solution.py:292
  66.2 19.7 %collective-permute-start.8 = (bf16[4,704,128]{2,1,0:T(8,128)(2,1)}, bf16[4,704,128]{2,1,0:T(8,128)(2,1)}, u32[]{:S(2)}, u32[]{:S(2)}) collective-permute-start(bf16[4,704,128]{2,1,0:T(8,128)(2,1)} %copy-done.5), channel_id=1, source_target_pairs={{0,4},{4,0},{1,5},{5,1},{2,6},{6,2},{3,7},{7,3},{8,12},{12,8},{9,1... | collective-permute-start | bytes 2162696 | tf_op jit(solution)/shard_map/ppermute | solution.py:292
  66.7 20.2 %collective-permute-start.6 = (bf16[4,704,128]{2,1,0:T(8,128)(2,1)}, bf16[4,704,128]{2,1,0:T(8,128)(2,1)}, u32[]{:S(2)}, u32[]{:S(2)}) collective-permute-start(bf16[4,704,128]{2,1,0:T(8,128)(2,1)} %collective-permute-done.5.refs_4_), channel_id=1, source_target_pairs={{0,4},{4,0},{1,5},{5,1},{2,6},{6,2},{3,7},{7,3},{8,12},{12,8},{9,1... | collective-permute-start | bytes 2162696 | tf_op jit(solution)/shard_map/ppermute | solution.py:292
  72.4 14.6 %collective-permute-start.12 = (bf16[4,704,128]{2,1,0:T(8,128)(2,1)}, bf16[4,704,128]{2,1,0:T(8,128)(2,1)}, u32[]{:S(2)}, u32[]{:S(2)}) collective-permute-start(bf16[4,704,128]{2,1,0:T(8,128)(2,1)} %collective-permute-done.11.refs_10_), channel_id=1, source_target_pairs={{0,4},{4,0},{1,5},{5,1},{2,6},{6,2},{3,7},{7,3},{8,12},{12,8},{9,1... | collective-permute-start | bytes 2162696 | tf_op jit(solution)/shard_map/ppermute | solution.py:292
  83.1 16.2 %collective-permute-start.10 = (bf16[4,704,128]{2,1,0:T(8,128)(2,1)}, bf16[4,704,128]{2,1,0:T(8,128)(2,1)S(1)}, u32[]{:S(2)}, u32[]{:S(2)}) collective-permute-start(bf16[4,704,128]{2,1,0:T(8,128)(2,1)} %collective-permute-done.9.refs_8_), channel_id=1, source_target_pairs={{0,4},{4,0},{1,5},{5,1},{2,6},{6,2},{3,7},{7,3},{8,12},{12,8},{9,1... | collective-permute-start | bytes 2162696 | tf_op jit(solution)/shard_map/ppermute | solution.py:292
  84.9 11.1 %collective-permute-start.18 = (bf16[2,704,128]{2,1,0:T(8,128)(2,1)}, bf16[2,704,128]{2,1,0:T(8,128)(2,1)}, u32[]{:S(2)}, u32[]{:S(2)}) collective-permute-start(bf16[2,704,128]{2,1,0:T(8,128)(2,1)} %slice.146), channel_id=1, source_target_pairs={{0,56},{8,0},{16,8},{24,16},{32,24},{40,32},{48,40},{56,48},{1,57}... | collective-permute-start | bytes 1081352 | tf_op jit(solution)/shard_map/ppermute | solution.py:292
  85.9 12.1 %collective-permute-start.17 = (bf16[2,704,128]{2,1,0:T(8,128)(2,1)}, bf16[2,704,128]{2,1,0:T(8,128)(2,1)}, u32[]{:S(2)}, u32[]{:S(2)}) collective-permute-start(bf16[2,704,128]{2,1,0:T(8,128)(2,1)} %slice.145), channel_id=1, source_target_pairs={{0,8},{8,16},{16,24},{24,32},{32,40},{40,48},{48,56},{56,0},{1,9},... | collective-permute-start | bytes 1081352 | tf_op jit(solution)/shard_map/ppermute | solution.py:292
  86.9 12.4 %collective-permute-start.16 = (bf16[4,704,128]{2,1,0:T(8,128)(2,1)}, bf16[4,704,128]{2,1,0:T(8,128)(2,1)S(1)}, u32[]{:S(2)}, u32[]{:S(2)}) collective-permute-start(bf16[4,704,128]{2,1,0:T(8,128)(2,1)} %collective-permute-done.15.refs_14_), channel_id=1, source_target_pairs={{0,4},{4,0},{1,5},{5,1},{2,6},{6,2},{3,7},{7,3},{8,12},{12,8},{9,1... | collective-permute-start | bytes 2162696 | tf_op jit(solution)/shard_map/ppermute | solution.py:292
  86.9 13.1 %collective-permute-start.14 = (bf16[4,704,128]{2,1,0:T(8,128)(2,1)}, bf16[4,704,128]{2,1,0:T(8,128)(2,1)S(1)}, u32[]{:S(2)}, u32[]{:S(2)}) collective-permute-start(bf16[4,704,128]{2,1,0:T(8,128)(2,1)} %collective-permute-done.13.refs_12_), channel_id=1, source_target_pairs={{0,4},{4,0},{1,5},{5,1},{2,6},{6,2},{3,7},{7,3},{8,12},{12,8},{9,1... | collective-permute-start | bytes 2162696 | tf_op jit(solution)/shard_map/ppermute | solution.py:292
  96.0 3.3 %collective-permute-start.20 = (bf16[2,704,128]{2,1,0:T(8,128)(2,1)}, bf16[2,704,128]{2,1,0:T(8,128)(2,1)}, u32[]{:S(2)}, u32[]{:S(2)}) collective-permute-start(bf16[2,704,128]{2,1,0:T(8,128)(2,1)} %collective-permute-done.18.refs_17_), channel_id=1, source_target_pairs={{0,4},{4,0},{1,5},{5,1},{2,6},{6,2},{3,7},{7,3},{8,12},{12,8},{9,1... | collective-permute-start | bytes 1081352 | tf_op jit(solution)/shard_map/ppermute | solution.py:292
  98.0 2.0 %collective-permute-start.19 = (bf16[2,704,128]{2,1,0:T(8,128)(2,1)}, bf16[2,704,128]{2,1,0:T(8,128)(2,1)}, u32[]{:S(2)}, u32[]{:S(2)}) collective-permute-start(bf16[2,704,128]{2,1,0:T(8,128)(2,1)} %collective-permute-done.17.refs_16_), channel_id=1, source_target_pairs={{0,4},{4,0},{1,5},{5,1},{2,6},{6,2},{3,7},{7,3},{8,12},{12,8},{9,1... | collective-permute-start | bytes 1081352 | tf_op jit(solution)/shard_map/ppermute | solution.py:292
  138.7 5.3 %collective-permute-start.21 = (bf16[4,1040,128]{2,1,0:T(8,128)(2,1)}, bf16[4,1040,128]{2,1,0:T(8,128)(2,1)S(1)}, u32[]{:S(2)}, u32[]{:S(2)}) collective-permute-start(bf16[4,1040,128]{2,1,0:T(8,128)(2,1)} %get-tuple-element.8), channel_id=1, source_target_pairs={{0,4},{4,0},{1,5},{5,1},{2,6},{6,2},{3,7},{7,3},{8,12},{12,8},{9,1... | collective-permute-start | bytes 3194888 | tf_op jit(solution)/shard_map/ppermute | solution.py:292
  139.1 13.9 %all-to-all-start.2 = ((f32[4,2,136,128]{3,2,1,0:T(8,128)}), f32[4,2,136,128]{3,2,1,0:T(8,128)S(1)}, u32[]{:S(2)}, u32[]{:S(2)}) async-start(f32[4,2,136,128]{3,2,1,0:T(8,128)} %get-tuple-element.9), calls=%async_computation.2 | async-start | bytes 1114112 | tf_op jit(solution)/shard_map/all_to_all | solution.py:298
  145.0 10.3 %collective-permute-start.22 = (bf16[1040,128]{1,0:T(8,128)(2,1)}, bf16[1040,128]{1,0:T(8,128)(2,1)S(1)}, u32[]{:S(2)}, u32[]{:S(2)}) collective-permute-start(bf16[1040,128]{1,0:T(8,128)(2,1)} %get-tuple-element.12), channel_id=1, source_target_pairs={{0,64},{64,128},{128,192},{192,0},{1,65},{65,129},{129,193},{193,1... | collective-permute-start | bytes 798728 | tf_op jit(solution)/shard_map/ppermute | solution.py:292
  145.0 14.7 %collective-permute-start.24 = (bf16[1040,128]{1,0:T(8,128)(2,1)}, bf16[1040,128]{1,0:T(8,128)(2,1)S(1)}, u32[]{:S(2)}, u32[]{:S(2)}) collective-permute-start(bf16[1040,128]{1,0:T(8,128)(2,1)} %get-tuple-element.13), channel_id=1, source_target_pairs={{0,192},{64,0},{128,64},{192,128},{1,193},{65,1},{129,65},{193,129... | collective-permute-start | bytes 798728 | tf_op jit(solution)/shard_map/ppermute | solution.py:292
  148.2 12.7 %collective-permute-start.23 = (bf16[1040,128]{1,0:T(8,128)(2,1)S(1)}, bf16[1040,128]{1,0:T(8,128)(2,1)}, u32[]{:S(2)}, u32[]{:S(2)}) collective-permute-start(bf16[1040,128]{1,0:T(8,128)(2,1)S(1)} %get-tuple-element.14), channel_id=1, source_target_pairs={{0,128},{64,192},{128,0},{192,64},{1,129},{65,193},{129,1},{193,65... | collective-permute-start | bytes 798728 | tf_op jit(solution)/shard_map/ppermute | solution.py:292
  164.4 34.5 %all-to-all-start.3 = ((f32[32,40,128]{2,1,0:T(8,128)}), f32[32,40,128]{2,1,0:T(8,128)S(1)}, u32[]{:S(2)}, u32[]{:S(2)}) async-start(f32[32,40,128]{2,1,0:T(8,128)} %concatenate.24), calls=%async_computation.3 | async-start | bytes 1310720 | tf_op jit(solution)/shard_map/all_to_all | solution.py:387
  180.0 8.4 %collective-permute-start.25 = (f32[4,136,128]{2,1,0:T(8,128)S(1)}, f32[4,136,128]{2,1,0:T(8,128)S(1)}, u32[]{:S(2)}, u32[]{:S(2)}) collective-permute-start(f32[4,136,128]{2,1,0:T(8,128)S(1)} %slice_bitcast_fusion.2), channel_id=1, source_target_pairs={{0,192},{64,128},{128,64},{192,0},{1,193},{65,129},{129,65},{193,1... | collective-permute-start | bytes 835592 | tf_op jit(solution)/shard_map/ppermute | solution.py:323
  (7 other events, 44.4 us)

commit v3 on v2

--- a/solution.py
+++ b/solution.py
@@ -18,6 +18,7 @@
 BLOCK = 128
 KB = 512
 STEPS = Z * Y * C * BLOCK // KB
+EARLY = (Z // 2 - 1) * Y
 UNROLL = 4
 GROUPS = 2
 ROWS = 16
@@ -32,7 +33,8 @@
 
 def column_place(info, column):
     pair, second = column // 2, column % 2
-    offset = jnp.where(second == 0, Z - pair, jnp.where(pair == 0, Z // 2, pair))
+    near = jnp.where(second == 0, Z - 1 - pair, pair + 1)
+    offset = jnp.where(pair == Z // 2 - 1, second * (Z // 2), near)
     return (info[2] + offset) % Z
 
 
@@ -62,10 +64,10 @@
     )
 
 
-def score_step(info, step, group, block, q_ref, lse_ref, iq_ref, w_ref, masses, logits, tops):
+def score_step(info, step, base, group, block, q_ref, lse_ref, iq_ref, w_ref, masses, logits, tops):
     heads, _, latent = q_ref.shape[1:]
     iheads = iq_ref.shape[1] // ROWS
-    needed, visible = step_facts(info, step, group)
+    needed, visible = step_facts(info, base + step, group)
 
     @pl.when(needed)
     def compute():
@@ -96,73 +98,104 @@
         logits[group, step] = jnp.full((ROWS, KB), far_below, f32)
 
 
-def column_copies(column_refs, cols, sems):
-    copies = []
-    for column, pieces in enumerate(column_refs):
-        group = []
-        for side, part in enumerate(pieces):
-            at = 0
-            for i, piece in enumerate(part):
-                size = piece.shape[0]
-                group.append(
-                    pltpu.make_async_copy(
-                        piece, cols.at[column, side, pl.ds(at, size)], sems.at[column, side, i]
-                    )
-                )
-                at += size
-        copies.append(group)
-    return copies
-
-
-def kernel(info, lse_ref, iq_ref, w_ref, iqt_ref, *refs):
-    query_refs, refs = refs[:GROUPS], refs[GROUPS:]
-    column_refs = [((refs[2 * k],), (refs[2 * k + 1],)) for k in range(Z - 1)]
-    far, refs = refs[2 * (Z - 1) : 2 * (Z - 1) + 4], refs[2 * (Z - 1) + 4 :]
-    column_refs.insert(1, ((far[0], far[1]), (far[2], far[3])))
-    rows_ref, kept_ref, sent_ref, q_all, masses, logits, tops, scales, key_grads, wg_ref = refs[:10]
-    cols, sems, q_sems = refs[10:]
-    latent = q_all.shape[-1]
+def arrivals(query_refs, column_refs, q_all, cols, sems, q_sems):
     per = q_all.shape[1] // X
-    iheads = iq_ref.shape[1] // ROWS
-    copies = column_copies(column_refs, cols, sems)
-    query_copies = [
+    queries = [
         pltpu.make_async_copy(
             source.at[x, pl.ds(0, per)], q_all.at[group, pl.ds(x * per, per)], q_sems.at[group, x]
         )
         for group, source in enumerate(query_refs)
         for x in range(X)
     ]
-    for copy in query_copies:
+    columns = [
+        pltpu.make_async_copy(ref, cols.at[i // C, i % C], sems.at[i // C, i % C])
+        for i, ref in enumerate(column_refs)
+    ]
+    for copy in queries + columns[: 2 * C]:
         copy.start()
-    for group in copies:
-        for copy in group:
-            copy.start()
+    return queries, columns
+
+
+def score_steps(info, base, columns, cols, q_all, lse_ref, iq_ref, w_ref, masses, logits, tops):
+    per_pair = 2 * C
+
+    def step(index, carried):
+        for pair in range(len(columns) // per_pair):
+
+            @pl.when(index == pair * Y)
+            def arrive():
+                for copy in columns[pair * per_pair : (pair + 1) * per_pair]:
+                    copy.wait()
+
+        block = functools.partial(step_block, cols, index)
+
+        def one_group(group, carried):
+            score_step(
+                info, index, base, group, block, q_all, lse_ref, iq_ref, w_ref, masses, logits, tops
+            )
+            return carried
+
+        return lax.fori_loop(0, GROUPS, one_group, carried)
+
+    lax.fori_loop(0, len(columns) // per_pair * Y, step, 0)
+
+
+def early_kernel(info, lse_ref, iq_ref, w_ref, *refs):
+    query_refs, column_refs, refs = refs[:GROUPS], refs[GROUPS:-8], refs[-8:]
+    masses, logits, tops, keys_ref, q_all, cols, sems, q_sems = refs
+    latent = q_all.shape[-1]
+    queries, columns = arrivals(query_refs, column_refs, q_all, cols, sems, q_sems)
+    tops[...] = jnp.full(tops.shape, far_below, f32)
+    for copy in queries:
+        copy.wait()
+    for copy in columns[2 * C :]:
+        copy.start()
+    score_steps(info, 0, columns, cols, q_all, lse_ref, iq_ref, w_ref, masses, logits, tops)
+
+    def keep_keys(step, carried):
+        keys_ref[step] = step_block(cols, step, latent, latent + BLOCK)
+        return carried
+
+    lax.fori_loop(0, EARLY, keep_keys, 0)
+
+
+def late_kernel(info, lse_ref, iq_ref, w_ref, iqt_ref, early_tops, *refs):
+    query_refs, column_refs, refs = refs[:GROUPS], refs[GROUPS : GROUPS + 2 * C], refs[GROUPS + 2 * C :]
+    early_refs, refs = refs[:3], refs[3:]
+    rows_ref, kept_ref, sent_ref, q_all, masses, logits, tops, scales, key_grads, wg_ref = refs[:10]
+    keys_all, cols, sems, q_sems, early_sems = refs[10:]
+    latent = q_all.shape[-1]
+    iheads = iq_ref.shape[1] // ROWS
+    queries, columns = arrivals(query_refs, column_refs, q_all, cols, sems, q_sems)
+    early_copies = [
+        pltpu.make_async_copy(source, target, early_sems.at[i])
+        for i, (source, target) in enumerate(
+            zip(
+                early_refs,
+                (
+                    masses.at[:, pl.ds(0, EARLY)],
+                    logits.at[:, pl.ds(0, EARLY)],
+                    keys_all.at[pl.ds(0, EARLY)],
+                ),
+            )
+        )
+    ]
     own_rows = iheads // X * ROWS
     rows_ref[...] = jnp.zeros(rows_ref.shape, f32)
     wg_ref[...] = jnp.zeros(wg_ref.shape, f32)
-    tops[...] = jnp.full(tops.shape, far_below, f32)
-    for copy in query_copies:
+    tops[...] = early_tops[...]
+    for copy in queries:
         copy.wait()
-
-    def first_step(step, carried):
-        for pair in range(Z // 2):
-
-            @pl.when(step == pair * Y)
-            def arrive():
-                for copy in copies[2 * pair] + copies[2 * pair + 1]:
-                    copy.wait()
-
-        block = functools.partial(step_block, cols, step)
-
-        def one_group(group, carried):
-            score_step(
-                info, step, group, block, q_all, lse_ref, iq_ref, w_ref, masses, logits, tops
-            )
-            return carried
-
-        return lax.fori_loop(0, GROUPS, one_group, carried)
-
-    lax.fori_loop(0, STEPS, first_step, 0)
+    for copy in early_copies:
+        copy.start()
+    score_steps(
+        info, EARLY, columns, cols, q_all, lse_ref, iq_ref, w_ref,
+        masses.at[:, pl.ds(EARLY, Y)], logits.at[:, pl.ds(EARLY, Y)], tops,
+    )
+    for step in range(Y):
+        keys_all[EARLY + step] = step_block(cols, step, latent, latent + BLOCK)
+    for copy in early_copies:
+        copy.wait()
 
     loss = jnp.float32(0.0)
     for group in range(GROUPS):
@@ -195,7 +228,7 @@
 
             @pl.when(needed)
             def compute():
-                keys = step_block(cols, kb, latent, latent + BLOCK)
+                keys = keys_all[kb]
                 target = masses[group, kb] * wide(scales[group, 0])
                 coefficient = logits[group, kb] * wide(scales[group, 1]) - target
                 coefficient = coefficient.astype(bf16).astype(f32)
@@ -258,34 +291,78 @@
 vmem_limit = 56 * 2**20
 
 
-def fused(info, lse, iq, w, queries, heads, columns, far):
-    piece = columns[0][0]
+def call(body, info, small, queries, heads, columns, more, out_shape, scratch, flops, name):
+    count = len(columns) // C
     latent = queries[0].shape[-1]
-    flat = [array for pair in columns for array in pair] + [a for pair in far for a in pair]
+    any_count = GROUPS + len(columns) + len(more)
     return pl.pallas_call(
-        kernel,
-        out_shape=(
+        body,
+        out_shape=out_shape,
+        in_specs=[smem_spec] + [vmem_spec] * len(small) + [any_spec] * any_count,
+        out_specs=(vmem_spec,) * len(out_shape),
+        scratch_shapes=[pltpu.VMEM((GROUPS, heads, ROWS, latent), bf16)]
+        + scratch
+        + [
+            pltpu.VMEM((count, C) + columns[0].shape, bf16),
+            pltpu.SemaphoreType.DMA((count, C)),
+            pltpu.SemaphoreType.DMA((GROUPS, X)),
+        ]
+        + ([pltpu.SemaphoreType.DMA((len(more),))] if more else []),
+        compiler_params=pltpu.CompilerParams(vmem_limit_bytes=vmem_limit),
+        cost_estimate=pl.CostEstimate(flops=flops, bytes_accessed=16 * 2**20, transcendentals=0),
+        name=name,
+    )(info, *small, *queries, *columns, *more)
+
+
+def fused(info, lse, iq, w, queries, heads, pairs):
+    flat = [array for pair in pairs for array in pair]
+    columns = flat[2 * C :] + flat[: 2 * C]
+    early_columns, late_columns = columns[: EARLY // Y * 2 * C], columns[EARLY // Y * 2 * C :]
+    step_flops = 2 * KB * (heads * GROUPS * ROWS * queries[0].shape[-1] + iq.size)
+    early = call(
+        early_kernel,
+        info,
+        (lse, iq, w),
+        queries,
+        heads,
+        early_columns,
+        (),
+        (
+            jax.ShapeDtypeStruct((GROUPS, EARLY, ROWS, KB), f32),
+            jax.ShapeDtypeStruct((GROUPS, EARLY, ROWS, KB), f32),
+            jax.ShapeDtypeStruct((GROUPS, ROWS, KB), f32),
+            jax.ShapeDtypeStruct((EARLY, BLOCK, KB), bf16),
+        ),
+        [],
+        EARLY * step_flops,
+        "early",
+    )
+    masses, logits, tops, keys = early
+    return call(
+        late_kernel,
+        info,
+        (lse, iq, w, jnp.swapaxes(iq, 1, 2), tops),
+        queries,
+        heads,
+        late_columns,
+        (masses, logits, keys),
+        (
             jax.ShapeDtypeStruct((X, GROUPS, iq.shape[1] // X + 8, BLOCK), f32),
             jax.ShapeDtypeStruct((Y, Z * BLOCK + LOSS_ROWS, BLOCK), bf16),
             jax.ShapeDtypeStruct((Y, Z * BLOCK + LOSS_ROWS, BLOCK), bf16),
         ),
-        in_specs=[smem_spec] + [vmem_spec] * 4 + [any_spec] * (len(flat) + GROUPS),
-        out_specs=(vmem_spec,) * 3,
-        scratch_shapes=[
-            pltpu.VMEM((GROUPS, heads, ROWS, latent), bf16),
+        [
             pltpu.VMEM((GROUPS, STEPS, ROWS, KB), f32),
             pltpu.VMEM((GROUPS, STEPS, ROWS, KB), f32),
             pltpu.VMEM((GROUPS, ROWS, KB), f32),
             pltpu.VMEM((GROUPS, 2, ROWS, BLOCK), f32),
             pltpu.VMEM((BLOCK, KB), f32),
             pltpu.VMEM(iq.shape, f32),
-            pltpu.VMEM((Z, C) + piece.shape, bf16),
-            pltpu.SemaphoreType.DMA((Z, C, 2)),
-            pltpu.SemaphoreType.DMA((GROUPS, X)),
+            pltpu.VMEM((STEPS, BLOCK, KB), bf16),
         ],
-        compiler_params=pltpu.CompilerParams(vmem_limit_bytes=vmem_limit),
-        name="fused",
-    )(info, lse, iq, w, jnp.swapaxes(iq, 1, 2), *queries, *flat)
+        Y * step_flops + 3 * STEPS * 2 * KB * iq.size,
+        "late",
+    )
 
 
 def ring(axis, size, offset):
@@ -322,15 +399,21 @@
     def mirror(array):
         return lax.ppermute(array, "y", [(i, Y - 1 - i) for i in range(Y)])
 
+    own = jnp.concatenate([latents, index_keys], axis=1).T
+    around = [ring("y", Y, -1)(own), ring("y", Y, 2)(own), ring("y", Y, 1)(own)]
+    column = jnp.stack([own] + around)
+    after = jnp.max(column[:, 0, :]) * 0.0
+
     extra = [index_queries.reshape(shard, -1)] + terms(main_lse) + terms(index_weights)
     used = sum(part.shape[1] for part in extra)
     more = -(-used // latent)
     extra.append(jnp.zeros((shard, more * latent - used), bf16))
     extra = jnp.concatenate(extra, axis=1).reshape(shard, more, latent)
+
     packed = jnp.concatenate([main_queries, extra], axis=1)
     packed = packed.reshape(GROUPS, X, ROWS, heads + more, latent)
     packed = jnp.swapaxes(packed, 2, 3)
-    packed = (head_exchange(packed[0]), head_exchange(mirror(packed[1])))
+    packed = (head_exchange(packed[0]), head_exchange(mirror(packed[1] + after)))
     extra = jnp.stack([part[:, heads:] for part in packed])
     extra = jnp.swapaxes(extra, 2, 3).reshape(GROUPS, X, ROWS, more * latent)
 
@@ -349,20 +432,15 @@
     lse = jnp.broadcast_to(lse, lse.shape[:2] + (BLOCK,))
     w = jnp.broadcast_to(w, w.shape[:2] + (BLOCK,))
 
-    own = jnp.concatenate([latents, index_keys], axis=1).T
-    column = jnp.stack(
-        [own, ring("y", Y, -1)(own), ring("y", Y, 2)(own), ring("y", Y, 1)(own)]
-    )
     columns = [column]
     above = below = column
     for _ in range(Z // 2 - 1):
         below, above = up(below), down(above)
         columns += [below, above]
-    far = (up(below[: Y // 2]), down(above[Y // 2 :]))
     pairs = [(array, swap(array)) for array in columns]
-    far = (far, tuple(swap(array) for array in far))
-
-    row_grads, kept, sent = fused(info, lse, iq, w, packed, heads * X, pairs, far)
+    pairs.insert(1, (up(below), down(pairs[-1][1])))
+
+    row_grads, kept, sent = fused(info, lse, iq, w, packed, heads * X, pairs)
 
     per = iheads * ROWS
     back = head_exchange(row_grads)
@@ -379,15 +457,16 @@
     parts = [(kept[i].astype(f32) + came[i].astype(f32)).astype(bf16) for i in range(Y)]
     parts = [parts[0]] + [ring("y", Y, i)(parts[i]) for i in range(1, Y)]
     part = sum(array.astype(f32) for array in parts)
-    loss = jnp.sum(part[Z * BLOCK, :]) + 0.0 * back[0, 0, 0, 0]
+    loss = part[Z * BLOCK, :] + 0.0 * back[0, 0, 0, 0]
     part = jnp.swapaxes(part[: Z * BLOCK].reshape(Z, BLOCK, BLOCK), 1, 2)
-    part = part.reshape(Z * X, rows, BLOCK)
-    loss = jnp.broadcast_to(loss, (Z * X, 8, BLOCK))
+    part = part.reshape(Z * X, rows, BLOCK).astype(bf16)
+    loss = jnp.pad(jnp.stack(terms(loss)), ((0, LOSS_ROWS - 3), (0, 0)))
+    loss = jnp.broadcast_to(loss, (Z * X, LOSS_ROWS, BLOCK))
     part = jnp.concatenate([part, loss], axis=1)
     part = lax.all_to_all(part, ("z", "head"), 0, 0, tiled=True)
-    part = jnp.sum(part, axis=0)
+    part = jnp.sum(part.astype(f32), axis=0)
     key_grads = part[:rows]
-    loss = part[rows, 0] / all_tokens
+    loss = jnp.sum(part[rows:]) / all_tokens
     return (loss, query_grads, weight_grads, key_grads)
 
 

time: 203 us -> 197 us (0.970)
  waiting for transfers between devices: 70.6 us -> 61 us
  other arithmetic: 6.95 us -> 12.6 us
  local copies, waits for them, and re-layouts: 22.7 us -> 17.9 us
  Pallas kernels: 36.3 us -> 40 us
    ppermute x24 -> x22, waiting for transfers between devices: 44 us -> 32.6 us  [ring(): lax.ppermute(array, axis, [(i, (i + offset) % size) for i in range(size)])]
    all_to_all x1, waiting for transfers between devices: 8.65 us -> 3.03 us  [per_device(): part = lax.all_to_all(part, ('z', 'head'), 0, 0, tiled=True)]
    ppermute x2, waiting for transfers between devices: 6.3 us -> 11.3 us  [mirror(): return lax.ppermute(array, 'y', [(i, Y - 1 - i) for i in range(Y)])]
    slice x4 -> x1, local copies, waits for them, and re-layouts: 4.54 us -> 0.51 us  [per_device(): loss = part[Z * BLOCK, :] + 0.0 * back[0, 0, 0, 0]]
    pallas_call x1 -> x2, Pallas kernels: 36.3 us -> 40 us  [call(): pl.pallas_call(body, out_shape=out_shape, in_specs=[smem_spec] + [vmem_sp...]
    all_to_all x1, starting transfers between devices: 15.6 us -> 18.2 us  [per_device(): part = lax.all_to_all(part, ('z', 'head'), 0, 0, tiled=True)]
    ppermute x24 -> x22, starting transfers between devices: 26.3 us -> 23.9 us  [ring(): lax.ppermute(array, axis, [(i, (i + offset) % size) for i in range(size)])]
    all_to_all x3, waiting for transfers between devices: 11.6 us -> 14 us  [head_exchange(): return lax.all_to_all(array, 'head', 0, 0, tiled=True)]
  transfers between devices with their start and end apart: 30 -> 28, of which waited for: 16 -> 11; matrix products, arithmetic and copies ran while one was open for 10% -> 9% of each run, Pallas kernels for 0% -> 9%
where the time goes in v3:
time: 197 us; the launch traced here: 195 us
  waiting for transfers between devices  61 us (31%)
  starting transfers between devices  59.8 us (30%)
  Pallas kernels  40 us (20%)
  local copies, waits for them, and re-layouts  17.9 us (9%)
  other arithmetic  12.6 us (6%)
  between operations  4.12 us (2%)
    pallas_call x2, Pallas kernels, call(): pl.pallas_call(body, out_shape=out_shape, in_specs=[smem_spec] + [vmem_sp...  40 us
    ppermute x22, waiting for transfers between devices, ring(): lax.ppermute(array, axis, [(i, (i + offset) % size) for i in range(size)])  32.6 us
    ppermute x22, starting transfers between devices, ring(): lax.ppermute(array, axis, [(i, (i + offset) % size) for i in range(size)])  23.9 us
    all_to_all x1, starting transfers between devices, per_device(): part = lax.all_to_all(part, ('z', 'head'), 0, 0, tiled=True)  18.2 us
    all_to_all x3, starting transfers between devices, head_exchange(): return lax.all_to_all(array, 'head', 0, 0, tiled=True)  14.7 us
    all_to_all x3, waiting for transfers between devices, head_exchange(): return lax.all_to_all(array, 'head', 0, 0, tiled=True)  14 us
    ppermute x2, waiting for transfers between devices, mirror(): return lax.ppermute(array, 'y', [(i, Y - 1 - i) for i in range(Y)])  11.3 us
    unnamed x20, local copies, waits for them, and re-layouts  7.9 us
  transfers between devices with their start and end apart: 28, of which 11 were waited for; matrix products, arithmetic and copies ran while one was open for 9% of the time, Pallas kernels for 9%

profile of v3, /device:TPU:2, one launch (start us, length us, event | category | flops | bytes accessed | tf_op | source)
XLA Modules:
  0.0 195.4 jit_solution(769001313973552159)
XLA Ops:
  1.5 1.6 fusion.7
  3.1 3.0 %collective-permute-start = (bf16[704,128]{1,0:T(8,128)(2,1)}, bf16[704,128]{1,0:T(8,128)(2,1)}, u32[]{:S(2)}, u32[]{:S(2)}) collective-permute-start(bf16[704,128]{1,0:T(8,128)(2,1)} %get-tuple-element.27), channel_id=1, source_target_pairs={{0,192},{64,0},{128,64},{192,128},{1,193},{65,1},{129,65},{193,129... | collective-permute-start | bytes 540680 | tf_op jit(solution)/shard_map/ppermute | solution.py:369
  11.4 3.9 %copy.38 = bf16[128,16,576]{2,1,0:T(8,128)(2,1)S(1)} copy(bf16[128,16,576]{0,2,1:T(8,128)(2,1)} %param.6) | data formatting | bytes 4718592 | tf_op args[0]
  16.4 1.5 collective-permute-done.2
  17.8 2.1 %pad_maximum_fusion.refs_2_ = bf16[4,704,128]{2,1,0:T(8,128)(2,1)} fusion(bf16[1,704,128]{2,1,0:T(8,128)(2,1)} %bitcast.13, bf16[1,704,128]{2,1,0:T(8,128)(2,1)} %bitcast.12, bf16[1,704,128]{2,1,0:T(8,128)(2,1)} %bitcast.11, bf16[1,704,128]{2,1,0:T(8,128)(2,1)S(1)} %get-tuple-element.26), kind=kLoop, calls=%fused_computation.5 | loop fusion | flops 1081344 | bytes 1441792 | tf_op jit(solution)/shard_map/stack | solution.py:404
  19.9 1.3 slice_reduce_fusion.3
  21.9 1.9 slice_bitcast_fusion
  24.5 4.8 %all-to-all-start = ((bf16[4,18,16,576]{3,2,1,0:T(8,128)(2,1)}), bf16[4,18,16,576]{3,2,1,0:T(8,128)(2,1)S(1)}, u32[]{:S(2)}, u32[]{:S(2)}) async-start(bf16[4,18,16,576]{3,2,1,0:T(8,128)(2,1)} %get-tuple-element.18), calls=%async_computation | async-start | bytes 2949120 | tf_op jit(solution)/shard_map/all_to_all | solution.py:375
  29.4 1.9 collective-permute-start.4
  31.3 3.9 %collective-permute-start.6 = (bf16[4,704,128]{2,1,0:T(8,128)(2,1)}, bf16[4,704,128]{2,1,0:T(8,128)(2,1)}, u32[]{:S(2)}, u32[]{:S(2)}) collective-permute-start(bf16[4,704,128]{2,1,0:T(8,128)(2,1)} %pad_maximum_fusion.refs_2_), channel_id=1, source_target_pairs={{0,56},{8,0},{16,8},{24,16},{32,24},{40,32},{48,40},{56,48},{1,57}... | collective-permute-start | bytes 2162696 | tf_op jit(solution)/shard_map/ppermute | solution.py:369
  35.2 15.3 %collective-permute-done.4.refs_2_ = bf16[4,704,128]{2,1,0:T(8,128)(2,1)} collective-permute-done((bf16[4,704,128]{2,1,0:T(8,128)(2,1)}, bf16[4,704,128]{2,1,0:T(8,128)(2,1)}, u32[]{:S(2)}, u32[]{:S(2)}) %collective-permute-start.4) | collective-permute-done | bytes 720928 | tf_op jit(solution)/shard_map/ppermute | solution.py:369
  50.5 3.2 %collective-permute-start.10 = (bf16[4,704,128]{2,1,0:T(8,128)(2,1)}, bf16[4,704,128]{2,1,0:T(8,128)(2,1)}, u32[]{:S(2)}, u32[]{:S(2)}) collective-permute-start(bf16[4,704,128]{2,1,0:T(8,128)(2,1)} %collective-permute-done.6.refs_4_), channel_id=1, source_target_pairs={{0,56},{8,0},{16,8},{24,16},{32,24},{40,32},{48,40},{56,48},{1,57}... | collective-permute-start | bytes 2162696 | tf_op jit(solution)/shard_map/ppermute | solution.py:369
  53.7 5.7 %collective-permute-done.3 = bf16[4,18,16,576]{3,2,1,0:T(8,128)(2,1)} collective-permute-done((bf16[4,18,16,576]{3,2,1,0:T(8,128)(2,1)}, bf16[4,18,16,576]{3,2,1,0:T(8,128)(2,1)}, u32[]{:S(2)}, u32[]{:S(2)}) %collective-permute-start.3) | collective-permute-done | bytes 1327136 | tf_op jit(solution)/shard_map/ppermute | solution.py:400
  59.5 4.8 %all-to-all-start.1 = ((bf16[4,18,16,576]{3,2,1,0:T(8,128)(2,1)}), bf16[4,18,16,576]{3,2,1,0:T(8,128)(2,1)S(1)}, u32[]{:S(2)}, u32[]{:S(2)}) async-start(bf16[4,18,16,576]{3,2,1,0:T(8,128)(2,1)} %collective-permute-done.3), calls=%async_computation.1 | async-start | bytes 2949120 | tf_op jit(solution)/shard_map/all_to_all | solution.py:375
  64.3 3.8 %collective-permute-done.8.refs_6_ = bf16[4,704,128]{2,1,0:T(8,128)(2,1)} collective-permute-done((bf16[4,704,128]{2,1,0:T(8,128)(2,1)}, bf16[4,704,128]{2,1,0:T(8,128)(2,1)}, u32[]{:S(2)}, u32[]{:S(2)}) %collective-permute-start.8) | collective-permute-done | bytes 720928 | tf_op jit(solution)/shard_map/ppermute | solution.py:369
  68.1 3.2 %collective-permute-start.14 = (bf16[4,704,128]{2,1,0:T(8,128)(2,1)}, bf16[4,704,128]{2,1,0:T(8,128)(2,1)}, u32[]{:S(2)}, u32[]{:S(2)}) collective-permute-start(bf16[4,704,128]{2,1,0:T(8,128)(2,1)} %collective-permute-done.10.refs_8_), channel_id=1, source_target_pairs={{0,56},{8,0},{16,8},{24,16},{32,24},{40,32},{48,40},{56,48},{1,57}... | collective-permute-start | bytes 2162696 | tf_op jit(solution)/shard_map/ppermute | solution.py:369
  72.8 9.1 %all-to-all-done.1.refs_1_ = bf16[4,18,16,576]{3,2,1,0:T(8,128)(2,1)S(1)} async-done(((bf16[4,18,16,576]{3,2,1,0:T(8,128)(2,1)}), bf16[4,18,16,576]{3,2,1,0:T(8,128)(2,1)S(1)}, u32[]{:S(2)}, u32[]{:S(2)}) %all-to-all-start.1) | async-done | bytes 1327136 | tf_op jit(solution)/shard_map/all_to_all | solution.py:375
  82.5 4.8 %collective-permute-done.12.refs_10_ = bf16[4,704,128]{2,1,0:T(8,128)(2,1)} collective-permute-done((bf16[4,704,128]{2,1,0:T(8,128)(2,1)}, bf16[4,704,128]{2,1,0:T(8,128)(2,1)}, u32[]{:S(2)}, u32[]{:S(2)}) %collective-permute-start.12) | collective-permute-done | bytes 720928 | tf_op jit(solution)/shard_map/ppermute | solution.py:369
  89.6 1.2 collective-permute-done.15.refs_13_
  90.8 2.1 %collective-permute-start.18 = (bf16[4,704,128]{2,1,0:T(8,128)(2,1)}, bf16[4,704,128]{2,1,0:T(8,128)(2,1)S(1)}, u32[]{:S(2)}, u32[]{:S(2)}) collective-permute-start(bf16[4,704,128]{2,1,0:T(8,128)(2,1)} %collective-permute-done.15.refs_13_), channel_id=1, source_target_pairs={{0,56},{8,0},{16,8},{24,16},{32,24},{40,32},{48,40},{56,48},{1,57}... | collective-permute-start | bytes 2162696 | tf_op jit(solution)/shard_map/ppermute | solution.py:369
  93.0 1.3 broadcast_in_dim.19.lse_ref
  95.3 17.7 %early.1 = (f32[2,12,16,512]{3,2,1,0:T(8,128)}, f32[2,12,16,512]{3,2,1,0:T(8,128)}, f32[2,16,512]{2,1,0:T(8,128)}, bf16[12,128,512]{2,1,0:T(8,128)(2,1)}) custom-call(s32[5]{0:T(128)} %stack.68.info, f32[2,1024,128]{2,1,0:T(8,128)} %broadcast_in_dim.19.lse_ref, bf16[2,512,128]{2,1,0:T(8,128)(2,1)} %bitcast.84, f32[2,512,128]{2,1,0:T(8,128)} %broadcast_in_dim.21.w_ref, ...), custom_call_target="tpu_custom_call" | custom-call | flops 16106127360 | bytes 16777216 | tf_op jit(solution)/shard_map/early/pallas_call | solution.py:298
  114.4 22.3 %late.1 = (f32[4,2,136,128]{3,2,1,0:T(8,128)}, bf16[4,1040,128]{2,1,0:T(8,128)(2,1)}, bf16[4,1040,128]{2,1,0:T(8,128)(2,1)}) custom-call(s32[5]{0:T(128)} %stack.68.info, f32[2,1024,128]{2,1,0:T(8,128)} %broadcast_in_dim.19.lse_ref, bf16[2,512,128]{2,1,0:T(8,128)(2,1)} %bitcast.85, f32[2,512,128]{2,1,0:T(8,128)} %broadcast_in_dim.21.w_ref, ...), custom_call_target="tpu_custom_call" | custom-call | flops 11811160064 | bytes 16777216 | tf_op jit(solution)/shard_map/late/pallas_call | solution.py:298
  136.9 5.0 %all-to-all-start.2 = ((f32[4,2,136,128]{3,2,1,0:T(8,128)}), f32[4,2,136,128]{3,2,1,0:T(8,128)S(1)}, u32[]{:S(2)}, u32[]{:S(2)}) async-start(f32[4,2,136,128]{3,2,1,0:T(8,128)} %get-tuple-element.17), calls=%async_computation.2 | async-start | bytes 1114112 | tf_op jit(solution)/shard_map/all_to_all | solution.py:375
  142.9 2.7 %collective-permute-start.21 = (bf16[1040,128]{1,0:T(8,128)(2,1)}, bf16[1040,128]{1,0:T(8,128)(2,1)S(1)}, u32[]{:S(2)}, u32[]{:S(2)}) collective-permute-start(bf16[1040,128]{1,0:T(8,128)(2,1)} %get-tuple-element.22), channel_id=1, source_target_pairs={{0,128},{64,192},{128,0},{192,64},{1,129},{65,193},{129,1},{193,65... | collective-permute-start | bytes 798728 | tf_op jit(solution)/shard_map/ppermute | solution.py:369
  146.2 4.9 %all-to-all-done.2 = f32[4,2,136,128]{3,2,1,0:T(8,128)S(1)} async-done(((f32[4,2,136,128]{3,2,1,0:T(8,128)}), f32[4,2,136,128]{3,2,1,0:T(8,128)S(1)}, u32[]{:S(2)}, u32[]{:S(2)}) %all-to-all-start.2) | async-done | bytes 557088 | tf_op jit(solution)/shard_map/all_to_all | solution.py:375
  152.3 6.2 %collective-permute-done.20 = bf16[1040,128]{1,0:T(8,128)(2,1)S(1)} collective-permute-done((bf16[1040,128]{1,0:T(8,128)(2,1)}, bf16[1040,128]{1,0:T(8,128)(2,1)S(1)}, u32[]{:S(2)}, u32[]{:S(2)}) %collective-permute-start.20) | collective-permute-done | bytes 266272 | tf_op jit(solution)/shard_map/ppermute | solution.py:369
  159.1 1.2 fusion.2
  161.4 18.2 %all-to-all-start.3 = ((bf16[32,48,128]{2,1,0:T(8,128)(2,1)}), bf16[32,48,128]{2,1,0:T(8,128)(2,1)S(1)}, u32[]{:S(2)}, u32[]{:S(2)}) async-start(bf16[32,48,128]{2,1,0:T(8,128)(2,1)} %pad_maximum_fusion.1), calls=%async_computation.3 | async-start | bytes 786432 | tf_op jit(solution)/shard_map/all_to_all | solution.py:466
  179.6 2.2 %collective-permute-start.23 = (f32[4,136,128]{2,1,0:T(8,128)S(1)}, f32[4,136,128]{2,1,0:T(8,128)S(1)}, u32[]{:S(2)}, u32[]{:S(2)}) collective-permute-start(f32[4,136,128]{2,1,0:T(8,128)S(1)} %slice_bitcast_fusion.1), channel_id=1, source_target_pairs={{0,192},{64,128},{128,64},{192,0},{1,193},{65,129},{129,65},{193,1... | collective-permute-start | bytes 835592 | tf_op jit(solution)/shard_map/ppermute | solution.py:400
  181.9 5.6 %collective-permute-done.23 = f32[4,136,128]{2,1,0:T(8,128)S(1)} collective-permute-done((f32[4,136,128]{2,1,0:T(8,128)S(1)}, f32[4,136,128]{2,1,0:T(8,128)S(1)}, u32[]{:S(2)}, u32[]{:S(2)}) %collective-permute-start.23) | collective-permute-done | bytes 278560 | tf_op jit(solution)/shard_map/ppermute | solution.py:400
  189.4 3.0 %all-to-all-done.3 = bf16[32,48,128]{2,1,0:T(8,128)(2,1)S(1)} async-done(((bf16[32,48,128]{2,1,0:T(8,128)(2,1)}), bf16[32,48,128]{2,1,0:T(8,128)(2,1)S(1)}, u32[]{:S(2)}, u32[]{:S(2)}) %all-to-all-start.3) | async-done | bytes 393248 | tf_op jit(solution)/shard_map/all_to_all | solution.py:466
  (108 shorter events, 21.8 us)
Async XLA Ops:
  3.1 13.2 %collective-permute-start = (bf16[704,128]{1,0:T(8,128)(2,1)}, bf16[704,128]{1,0:T(8,128)(2,1)}, u32[]{:S(2)}, u32[]{:S(2)}) collective-permute-start(bf16[704,128]{1,0:T(8,128)(2,1)} %get-tuple-element.27), channel_id=1, source_target_pairs={{0,192},{64,0},{128,64},{192,128},{1,193},{65,1},{129,65},{193,129... | collective-permute-start | bytes 540680 | tf_op jit(solution)/shard_map/ppermute | solution.py:369
  6.1 10.2 %collective-permute-start.1 = (bf16[704,128]{1,0:T(8,128)(2,1)}, bf16[704,128]{1,0:T(8,128)(2,1)}, u32[]{:S(2)}, u32[]{:S(2)}) collective-permute-start(bf16[704,128]{1,0:T(8,128)(2,1)} %get-tuple-element.27), channel_id=1, source_target_pairs={{0,128},{64,192},{128,0},{192,64},{1,129},{65,193},{129,1},{193,65... | collective-permute-start | bytes 540680 | tf_op jit(solution)/shard_map/ppermute | solution.py:369
  6.8 11.1 %collective-permute-start.2 = (bf16[704,128]{1,0:T(8,128)(2,1)}, bf16[704,128]{1,0:T(8,128)(2,1)}, u32[]{:S(2)}, u32[]{:S(2)}) collective-permute-start(bf16[704,128]{1,0:T(8,128)(2,1)} %get-tuple-element.27), channel_id=1, source_target_pairs={{0,64},{64,128},{128,192},{192,0},{1,65},{65,129},{129,193},{193,1... | collective-permute-start | bytes 540680 | tf_op jit(solution)/shard_map/ppermute | solution.py:369
  23.7 35.7 %collective-permute-start.3 = (bf16[4,18,16,576]{3,2,1,0:T(8,128)(2,1)}, bf16[4,18,16,576]{3,2,1,0:T(8,128)(2,1)}, u32[]{:S(2)}, u32[]{:S(2)}) collective-permute-start(bf16[4,18,16,576]{3,2,1,0:T(8,128)(2,1)} %get-tuple-element.19), channel_id=1, source_target_pairs={{0,192},{64,128},{128,64},{192,0},{1,193},{65,129},{129,65},{193,1... | collective-permute-start | bytes 3981320 | tf_op jit(solution)/shard_map/ppermute | solution.py:400
  24.5 29.2 %all-to-all-start = ((bf16[4,18,16,576]{3,2,1,0:T(8,128)(2,1)}), bf16[4,18,16,576]{3,2,1,0:T(8,128)(2,1)S(1)}, u32[]{:S(2)}, u32[]{:S(2)}) async-start(bf16[4,18,16,576]{3,2,1,0:T(8,128)(2,1)} %get-tuple-element.18), calls=%async_computation | async-start | bytes 2949120 | tf_op jit(solution)/shard_map/all_to_all | solution.py:375
  29.4 21.1 %collective-permute-start.4 = (bf16[4,704,128]{2,1,0:T(8,128)(2,1)}, bf16[4,704,128]{2,1,0:T(8,128)(2,1)}, u32[]{:S(2)}, u32[]{:S(2)}) collective-permute-start(bf16[4,704,128]{2,1,0:T(8,128)(2,1)} %pad_maximum_fusion.refs_2_), channel_id=1, source_target_pairs={{0,8},{8,16},{16,24},{24,32},{32,40},{40,48},{48,56},{56,0},{1,9},... | collective-permute-start | bytes 2162696 | tf_op jit(solution)/shard_map/ppermute | solution.py:369
  31.3 19.2 %collective-permute-start.6 = (bf16[4,704,128]{2,1,0:T(8,128)(2,1)}, bf16[4,704,128]{2,1,0:T(8,128)(2,1)}, u32[]{:S(2)}, u32[]{:S(2)}) collective-permute-start(bf16[4,704,128]{2,1,0:T(8,128)(2,1)} %pad_maximum_fusion.refs_2_), channel_id=1, source_target_pairs={{0,56},{8,0},{16,8},{24,16},{32,24},{40,32},{48,40},{56,48},{1,57}... | collective-permute-start | bytes 2162696 | tf_op jit(solution)/shard_map/ppermute | solution.py:369
  50.5 17.6 %collective-permute-start.8 = (bf16[4,704,128]{2,1,0:T(8,128)(2,1)}, bf16[4,704,128]{2,1,0:T(8,128)(2,1)}, u32[]{:S(2)}, u32[]{:S(2)}) collective-permute-start(bf16[4,704,128]{2,1,0:T(8,128)(2,1)} %collective-permute-done.4.refs_2_), channel_id=1, source_target_pairs={{0,8},{8,16},{16,24},{24,32},{32,40},{40,48},{48,56},{56,0},{1,9},... | collective-permute-start | bytes 2162696 | tf_op jit(solution)/shard_map/ppermute | solution.py:369
  50.5 17.6 %collective-permute-start.10 = (bf16[4,704,128]{2,1,0:T(8,128)(2,1)}, bf16[4,704,128]{2,1,0:T(8,128)(2,1)}, u32[]{:S(2)}, u32[]{:S(2)}) collective-permute-start(bf16[4,704,128]{2,1,0:T(8,128)(2,1)} %collective-permute-done.6.refs_4_), channel_id=1, source_target_pairs={{0,56},{8,0},{16,8},{24,16},{32,24},{40,32},{48,40},{56,48},{1,57}... | collective-permute-start | bytes 2162696 | tf_op jit(solution)/shard_map/ppermute | solution.py:369
  53.7 18.2 %copy-start = (bf16[4,18,16,576]{3,2,1,0:T(8,128)(2,1)}, bf16[4,18,16,576]{3,2,1,0:T(8,128)(2,1)S(1)}, u32[]{:S(2)}) copy-start(bf16[4,18,16,576]{3,2,1,0:T(8,128)(2,1)S(1)} %all-to-all-done.refs_0_) | copy-start | bytes 3981316
  59.5 22.4 %all-to-all-start.1 = ((bf16[4,18,16,576]{3,2,1,0:T(8,128)(2,1)}), bf16[4,18,16,576]{3,2,1,0:T(8,128)(2,1)S(1)}, u32[]{:S(2)}, u32[]{:S(2)}) async-start(bf16[4,18,16,576]{3,2,1,0:T(8,128)(2,1)} %collective-permute-done.3), calls=%async_computation.1 | async-start | bytes 2949120 | tf_op jit(solution)/shard_map/all_to_all | solution.py:375
  64.3 18.1 %collective-permute-start.5 = (bf16[4,704,128]{2,1,0:T(8,128)(2,1)}, bf16[4,704,128]{2,1,0:T(8,128)(2,1)}, u32[]{:S(2)}, u32[]{:S(2)}) collective-permute-start(bf16[4,704,128]{2,1,0:T(8,128)(2,1)} %collective-permute-done.4.refs_2_), channel_id=1, source_target_pairs={{0,4},{4,0},{1,5},{5,1},{2,6},{6,2},{3,7},{7,3},{8,12},{12,8},{9,1... | collective-permute-start | bytes 2162696 | tf_op jit(solution)/shard_map/ppermute | solution.py:369
  68.1 19.2 %collective-permute-start.12 = (bf16[4,704,128]{2,1,0:T(8,128)(2,1)}, bf16[4,704,128]{2,1,0:T(8,128)(2,1)}, u32[]{:S(2)}, u32[]{:S(2)}) collective-permute-start(bf16[4,704,128]{2,1,0:T(8,128)(2,1)} %collective-permute-done.8.refs_6_), channel_id=1, source_target_pairs={{0,8},{8,16},{16,24},{24,32},{32,40},{40,48},{48,56},{56,0},{1,9},... | collective-permute-start | bytes 2162696 | tf_op jit(solution)/shard_map/ppermute | solution.py:369
  68.1 19.2 %collective-permute-start.14 = (bf16[4,704,128]{2,1,0:T(8,128)(2,1)}, bf16[4,704,128]{2,1,0:T(8,128)(2,1)}, u32[]{:S(2)}, u32[]{:S(2)}) collective-permute-start(bf16[4,704,128]{2,1,0:T(8,128)(2,1)} %collective-permute-done.10.refs_8_), channel_id=1, source_target_pairs={{0,56},{8,0},{16,8},{24,16},{32,24},{40,32},{48,40},{56,48},{1,57}... | collective-permute-start | bytes 2162696 | tf_op jit(solution)/shard_map/ppermute | solution.py:369
  72.0 17.6 %collective-permute-start.7 = (bf16[4,704,128]{2,1,0:T(8,128)(2,1)}, bf16[4,704,128]{2,1,0:T(8,128)(2,1)}, u32[]{:S(2)}, u32[]{:S(2)}) collective-permute-start(bf16[4,704,128]{2,1,0:T(8,128)(2,1)} %collective-permute-done.6.refs_4_), channel_id=1, source_target_pairs={{0,4},{4,0},{1,5},{5,1},{2,6},{6,2},{3,7},{7,3},{8,12},{12,8},{9,1... | collective-permute-start | bytes 2162696 | tf_op jit(solution)/shard_map/ppermute | solution.py:369
  72.0 17.6 %collective-permute-start.11 = (bf16[4,704,128]{2,1,0:T(8,128)(2,1)}, bf16[4,704,128]{2,1,0:T(8,128)(2,1)}, u32[]{:S(2)}, u32[]{:S(2)}) collective-permute-start(bf16[4,704,128]{2,1,0:T(8,128)(2,1)} %collective-permute-done.10.refs_8_), channel_id=1, source_target_pairs={{0,4},{4,0},{1,5},{5,1},{2,6},{6,2},{3,7},{7,3},{8,12},{12,8},{9,1... | collective-permute-start | bytes 2162696 | tf_op jit(solution)/shard_map/ppermute | solution.py:369
  81.8 6.1 %copy-start.1 = (bf16[4,18,16,576]{3,2,1,0:T(8,128)(2,1)}, bf16[4,18,16,576]{3,2,1,0:T(8,128)(2,1)S(1)}, u32[]{:S(2)}) copy-start(bf16[4,18,16,576]{3,2,1,0:T(8,128)(2,1)S(1)} %all-to-all-done.1.refs_1_) | copy-start | bytes 3981316
  82.4 10.5 %collective-permute-start.9 = (bf16[4,704,128]{2,1,0:T(8,128)(2,1)}, bf16[4,704,128]{2,1,0:T(8,128)(2,1)}, u32[]{:S(2)}, u32[]{:S(2)}) collective-permute-start(bf16[4,704,128]{2,1,0:T(8,128)(2,1)} %collective-permute-done.8.refs_6_), channel_id=1, source_target_pairs={{0,4},{4,0},{1,5},{5,1},{2,6},{6,2},{3,7},{7,3},{8,12},{12,8},{9,1... | collective-permute-start | bytes 2162696 | tf_op jit(solution)/shard_map/ppermute | solution.py:369
  87.3 5.7 %collective-permute-start.13 = (bf16[4,704,128]{2,1,0:T(8,128)(2,1)}, bf16[4,704,128]{2,1,0:T(8,128)(2,1)}, u32[]{:S(2)}, u32[]{:S(2)}) collective-permute-start(bf16[4,704,128]{2,1,0:T(8,128)(2,1)} %collective-permute-done.12.refs_10_), channel_id=1, source_target_pairs={{0,4},{4,0},{1,5},{5,1},{2,6},{6,2},{3,7},{7,3},{8,12},{12,8},{9,1... | collective-permute-start | bytes 2162696 | tf_op jit(solution)/shard_map/ppermute | solution.py:369
  87.3 3.6 %collective-permute-start.15 = (bf16[4,704,128]{2,1,0:T(8,128)(2,1)}, bf16[4,704,128]{2,1,0:T(8,128)(2,1)}, u32[]{:S(2)}, u32[]{:S(2)}) collective-permute-start(bf16[4,704,128]{2,1,0:T(8,128)(2,1)} %collective-permute-done.14.refs_12_), channel_id=1, source_target_pairs={{0,4},{4,0},{1,5},{5,1},{2,6},{6,2},{3,7},{7,3},{8,12},{12,8},{9,1... | collective-permute-start | bytes 2162696 | tf_op jit(solution)/shard_map/ppermute | solution.py:369
  87.9 7.4 %copy-start.3 = (bf16[2,4,8,16,128]{4,3,2,1,0:T(8,128)(2,1)}, bf16[2,4,8,16,128]{4,3,2,1,0:T(8,128)(2,1)S(1)}, u32[]{:S(2)}) copy-start(bf16[2,4,8,16,128]{4,3,2,1,0:T(8,128)(2,1)S(1)} %copy.50) | copy-start | bytes 786436
  89.5 23.5 %collective-permute-start.16 = (bf16[4,704,128]{2,1,0:T(8,128)(2,1)}, bf16[4,704,128]{2,1,0:T(8,128)(2,1)S(1)}, u32[]{:S(2)}, u32[]{:S(2)}) collective-permute-start(bf16[4,704,128]{2,1,0:T(8,128)(2,1)} %pad_maximum_fusion.refs_2_), channel_id=1, source_target_pairs={{0,4},{4,0},{1,5},{5,1},{2,6},{6,2},{3,7},{7,3},{8,12},{12,8},{9,1... | collective-permute-start | bytes 2162696 | tf_op jit(solution)/shard_map/ppermute | solution.py:369
  89.6 23.5 %collective-permute-start.17 = (bf16[4,704,128]{2,1,0:T(8,128)(2,1)}, bf16[4,704,128]{2,1,0:T(8,128)(2,1)S(1)}, u32[]{:S(2)}, u32[]{:S(2)}) collective-permute-start(bf16[4,704,128]{2,1,0:T(8,128)(2,1)} %collective-permute-done.12.refs_10_), channel_id=1, source_target_pairs={{0,8},{8,16},{16,24},{24,32},{32,40},{40,48},{48,56},{56,0},{1,9},... | collective-permute-start | bytes 2162696 | tf_op jit(solution)/shard_map/ppermute | solution.py:369
  90.8 22.2 %collective-permute-start.18 = (bf16[4,704,128]{2,1,0:T(8,128)(2,1)}, bf16[4,704,128]{2,1,0:T(8,128)(2,1)S(1)}, u32[]{:S(2)}, u32[]{:S(2)}) collective-permute-start(bf16[4,704,128]{2,1,0:T(8,128)(2,1)} %collective-permute-done.15.refs_13_), channel_id=1, source_target_pairs={{0,56},{8,0},{16,8},{24,16},{32,24},{40,32},{48,40},{56,48},{1,57}... | collective-permute-start | bytes 2162696 | tf_op jit(solution)/shard_map/ppermute | solution.py:369
  136.8 5.2 %copy-start.2 = (bf16[4,1040,128]{2,1,0:T(8,128)(2,1)S(1)}, bf16[4,1040,128]{2,1,0:T(8,128)(2,1)}, u32[]{:S(2)}) copy-start(bf16[4,1040,128]{2,1,0:T(8,128)(2,1)} %get-tuple-element.15) | copy-start | bytes 3194884
  136.8 5.1 %collective-permute-start.19 = (bf16[4,1040,128]{2,1,0:T(8,128)(2,1)}, bf16[4,1040,128]{2,1,0:T(8,128)(2,1)S(1)}, u32[]{:S(2)}, u32[]{:S(2)}) collective-permute-start(bf16[4,1040,128]{2,1,0:T(8,128)(2,1)} %get-tuple-element.16), channel_id=1, source_target_pairs={{0,4},{4,0},{1,5},{5,1},{2,6},{6,2},{3,7},{7,3},{8,12},{12,8},{9,1... | collective-permute-start | bytes 3194888 | tf_op jit(solution)/shard_map/ppermute | solution.py:369
  136.9 14.2 %all-to-all-start.2 = ((f32[4,2,136,128]{3,2,1,0:T(8,128)}), f32[4,2,136,128]{3,2,1,0:T(8,128)S(1)}, u32[]{:S(2)}, u32[]{:S(2)}) async-start(f32[4,2,136,128]{3,2,1,0:T(8,128)} %get-tuple-element.17), calls=%async_computation.2 | async-start | bytes 1114112 | tf_op jit(solution)/shard_map/all_to_all | solution.py:375
  142.9 15.5 %collective-permute-start.20 = (bf16[1040,128]{1,0:T(8,128)(2,1)}, bf16[1040,128]{1,0:T(8,128)(2,1)S(1)}, u32[]{:S(2)}, u32[]{:S(2)}) collective-permute-start(bf16[1040,128]{1,0:T(8,128)(2,1)} %get-tuple-element.20), channel_id=1, source_target_pairs={{0,64},{64,128},{128,192},{192,0},{1,65},{65,129},{129,193},{193,1... | collective-permute-start | bytes 798728 | tf_op jit(solution)/shard_map/ppermute | solution.py:369
  142.9 15.5 %collective-permute-start.21 = (bf16[1040,128]{1,0:T(8,128)(2,1)}, bf16[1040,128]{1,0:T(8,128)(2,1)S(1)}, u32[]{:S(2)}, u32[]{:S(2)}) collective-permute-start(bf16[1040,128]{1,0:T(8,128)(2,1)} %get-tuple-element.22), channel_id=1, source_target_pairs={{0,128},{64,192},{128,0},{192,64},{1,129},{65,193},{129,1},{193,65... | collective-permute-start | bytes 798728 | tf_op jit(solution)/shard_map/ppermute | solution.py:369
  145.6 13.6 %collective-permute-start.22 = (bf16[1040,128]{1,0:T(8,128)(2,1)S(1)}, bf16[1040,128]{1,0:T(8,128)(2,1)}, u32[]{:S(2)}, u32[]{:S(2)}) collective-permute-start(bf16[1040,128]{1,0:T(8,128)(2,1)S(1)} %get-tuple-element.21), channel_id=1, source_target_pairs={{0,192},{64,0},{128,64},{192,128},{1,193},{65,1},{129,65},{193,129... | collective-permute-start | bytes 798728 | tf_op jit(solution)/shard_map/ppermute | solution.py:369
  161.4 31.0 %all-to-all-start.3 = ((bf16[32,48,128]{2,1,0:T(8,128)(2,1)}), bf16[32,48,128]{2,1,0:T(8,128)(2,1)S(1)}, u32[]{:S(2)}, u32[]{:S(2)}) async-start(bf16[32,48,128]{2,1,0:T(8,128)(2,1)} %pad_maximum_fusion.1), calls=%async_computation.3 | async-start | bytes 786432 | tf_op jit(solution)/shard_map/all_to_all | solution.py:466
  179.6 7.9 %collective-permute-start.23 = (f32[4,136,128]{2,1,0:T(8,128)S(1)}, f32[4,136,128]{2,1,0:T(8,128)S(1)}, u32[]{:S(2)}, u32[]{:S(2)}) collective-permute-start(f32[4,136,128]{2,1,0:T(8,128)S(1)} %slice_bitcast_fusion.1), channel_id=1, source_target_pairs={{0,192},{64,128},{128,64},{192,0},{1,193},{65,129},{129,65},{193,1... | collective-permute-start | bytes 835592 | tf_op jit(solution)/shard_map/ppermute | solution.py:400
  (4 other events, 4.0 us)

commit v4 on v3

--- a/solution.py
+++ b/solution.py
@@ -140,11 +140,20 @@
     lax.fori_loop(0, len(columns) // per_pair * Y, step, 0)
 
 
-def early_kernel(info, lse_ref, iq_ref, w_ref, *refs):
-    query_refs, column_refs, refs = refs[:GROUPS], refs[GROUPS:-8], refs[-8:]
-    masses, logits, tops, keys_ref, q_all, cols, sems, q_sems = refs
+def spread(source, target):
+    for group in range(GROUPS):
+        for i in range(source.shape[1]):
+            block = jnp.broadcast_to(source[group, i : i + 1, :], (BLOCK, BLOCK))
+            target[group, i * BLOCK : (i + 1) * BLOCK, :] = block.T
+
+
+def early_kernel(info, lse_in, iq_ref, w_in, *refs):
+    query_refs, column_refs, refs = refs[:GROUPS], refs[GROUPS:-10], refs[-10:]
+    masses, logits, tops, keys_ref, q_all, lse_ref, w_ref, cols, sems, q_sems = refs
     latent = q_all.shape[-1]
     queries, columns = arrivals(query_refs, column_refs, q_all, cols, sems, q_sems)
+    spread(lse_in, lse_ref)
+    spread(w_in, w_ref)
     tops[...] = jnp.full(tops.shape, far_below, f32)
     for copy in queries:
         copy.wait()
@@ -159,11 +168,11 @@
     lax.fori_loop(0, EARLY, keep_keys, 0)
 
 
-def late_kernel(info, lse_ref, iq_ref, w_ref, iqt_ref, early_tops, *refs):
+def late_kernel(info, lse_in, iq_ref, w_in, iqt_ref, early_tops, *refs):
     query_refs, column_refs, refs = refs[:GROUPS], refs[GROUPS : GROUPS + 2 * C], refs[GROUPS + 2 * C :]
     early_refs, refs = refs[:3], refs[3:]
     rows_ref, kept_ref, sent_ref, q_all, masses, logits, tops, scales, key_grads, wg_ref = refs[:10]
-    keys_all, cols, sems, q_sems, early_sems = refs[10:]
+    keys_all, lse_ref, w_ref, cols, sems, q_sems, early_sems = refs[10:]
     latent = q_all.shape[-1]
     iheads = iq_ref.shape[1] // ROWS
     queries, columns = arrivals(query_refs, column_refs, q_all, cols, sems, q_sems)
@@ -183,6 +192,8 @@
     own_rows = iheads // X * ROWS
     rows_ref[...] = jnp.zeros(rows_ref.shape, f32)
     wg_ref[...] = jnp.zeros(wg_ref.shape, f32)
+    spread(lse_in, lse_ref)
+    spread(w_in, w_ref)
     tops[...] = early_tops[...]
     for copy in queries:
         copy.wait()
@@ -319,6 +330,10 @@
     columns = flat[2 * C :] + flat[: 2 * C]
     early_columns, late_columns = columns[: EARLY // Y * 2 * C], columns[EARLY // Y * 2 * C :]
     step_flops = 2 * KB * (heads * GROUPS * ROWS * queries[0].shape[-1] + iq.size)
+    spaces = [
+        pltpu.VMEM((GROUPS, heads * ROWS, BLOCK), f32),
+        pltpu.VMEM(iq.shape, f32),
+    ]
     early = call(
         early_kernel,
         info,
@@ -333,7 +348,7 @@
             jax.ShapeDtypeStruct((GROUPS, ROWS, KB), f32),
             jax.ShapeDtypeStruct((EARLY, BLOCK, KB), bf16),
         ),
-        [],
+        spaces,
         EARLY * step_flops,
         "early",
     )
@@ -359,7 +374,8 @@
             pltpu.VMEM((BLOCK, KB), f32),
             pltpu.VMEM(iq.shape, f32),
             pltpu.VMEM((STEPS, BLOCK, KB), bf16),
-        ],
+        ]
+        + spaces,
         Y * step_flops + 3 * STEPS * 2 * KB * iq.size,
         "late",
     )
@@ -421,7 +437,7 @@
         part = extra[..., first : first + 3 * count].astype(f32)
         part = part.reshape(GROUPS, X, ROWS, 3, count)
         part = part[..., 0, :] + part[..., 1, :] + part[..., 2, :]
-        part = jnp.swapaxes(part, 2, 3).reshape(GROUPS, -1, 1)
+        part = jnp.swapaxes(part, 2, 3).reshape(GROUPS, -1, BLOCK)
         return part
 
     size = iheads * BLOCK
@@ -429,8 +445,6 @@
     iq = jnp.swapaxes(iq, 2, 3).reshape(GROUPS, -1, BLOCK)
     lse = column_of(size, heads) * log2e
     w = column_of(size + 3 * heads, iheads)
-    lse = jnp.broadcast_to(lse, lse.shape[:2] + (BLOCK,))
-    w = jnp.broadcast_to(w, w.shape[:2] + (BLOCK,))
 
     columns = [column]
     above = below = column

time: 197 us -> 195 us (0.990)
    broadcast_in_dim x3 -> x0, local copies, waits for them, and re-layouts: 2.42 us -> none  [the longest x1 1.34 us: per_device(): lse = jnp.broadcast_to(lse, lse.shape[:2] + (BLOCK,))]
  transfers between devices with their start and end apart: 28 -> 28, of which waited for: 11 -> 10; matrix products, arithmetic and copies ran while one was open for 9% -> 8% of each run, Pallas kernels for 9% -> 9%
where the time goes in v4:
time: 195 us; the launch traced here: 193 us
  starting transfers between devices  61.3 us (31%)
  waiting for transfers between devices  59.5 us (31%)
  Pallas kernels  39.1 us (20%)
  local copies, waits for them, and re-layouts  16.7 us (9%)
  other arithmetic  12.6 us (6%)
  between operations  4.12 us (2%)
    pallas_call x2, Pallas kernels, call(): pl.pallas_call(body, out_shape=out_shape, in_specs=[smem_spec] + [vmem_sp...  39.1 us
    ppermute x22, waiting for transfers between devices, ring(): lax.ppermute(array, axis, [(i, (i + offset) % size) for i in range(size)])  31.5 us
    ppermute x22, starting transfers between devices, ring(): lax.ppermute(array, axis, [(i, (i + offset) % size) for i in range(size)])  25 us
    all_to_all x1, starting transfers between devices, per_device(): part = lax.all_to_all(part, ('z', 'head'), 0, 0, tiled=True)  18.7 us
    all_to_all x3, starting transfers between devices, head_exchange(): return lax.all_to_all(array, 'head', 0, 0, tiled=True)  14.6 us
    all_to_all x3, waiting for transfers between devices, head_exchange(): return lax.all_to_all(array, 'head', 0, 0, tiled=True)  13.7 us
    ppermute x2, waiting for transfers between devices, mirror(): return lax.ppermute(array, 'y', [(i, Y - 1 - i) for i in range(Y)])  11.3 us
    unnamed x20, local copies, waits for them, and re-layouts  7.84 us
  transfers between devices with their start and end apart: 28, of which 10 were waited for; matrix products, arithmetic and copies ran while one was open for 8% of the time, Pallas kernels for 9%

profile of v4, /device:TPU:2, one launch (start us, length us, event | category | flops | bytes accessed | tf_op | source)
XLA Modules:
  0.0 193.3 jit_solution(14503261835683239297)
XLA Ops:
  1.5 1.6 fusion.7
  3.1 3.0 %collective-permute-start = (bf16[704,128]{1,0:T(8,128)(2,1)}, bf16[704,128]{1,0:T(8,128)(2,1)}, u32[]{:S(2)}, u32[]{:S(2)}) collective-permute-start(bf16[704,128]{1,0:T(8,128)(2,1)} %get-tuple-element.27), channel_id=1, source_target_pairs={{0,192},{64,0},{128,64},{192,128},{1,193},{65,1},{129,65},{193,129... | collective-permute-start | bytes 540680 | tf_op jit(solution)/shard_map/ppermute | solution.py:385
  9.9 1.0 copy.42
  11.4 3.9 %copy.21 = bf16[128,16,576]{2,1,0:T(8,128)(2,1)S(1)} copy(bf16[128,16,576]{0,2,1:T(8,128)(2,1)} %param.6) | data formatting | bytes 4718592 | tf_op args[0]
  16.4 1.5 collective-permute-done.2
  17.8 2.1 %pad_maximum_fusion.refs_2_ = bf16[4,704,128]{2,1,0:T(8,128)(2,1)} fusion(bf16[1,704,128]{2,1,0:T(8,128)(2,1)} %bitcast.13, bf16[1,704,128]{2,1,0:T(8,128)(2,1)} %bitcast.12, bf16[1,704,128]{2,1,0:T(8,128)(2,1)} %bitcast.11, bf16[1,704,128]{2,1,0:T(8,128)(2,1)S(1)} %get-tuple-element.26), kind=kLoop, calls=%fused_computation.5 | loop fusion | flops 1081344 | bytes 1441792 | tf_op jit(solution)/shard_map/stack | solution.py:420
  19.9 1.3 slice_reduce_fusion.3
  21.9 1.9 slice_bitcast_fusion
  24.5 4.8 %all-to-all-start = ((bf16[4,18,16,576]{3,2,1,0:T(8,128)(2,1)}), bf16[4,18,16,576]{3,2,1,0:T(8,128)(2,1)S(1)}, u32[]{:S(2)}, u32[]{:S(2)}) async-start(bf16[4,18,16,576]{3,2,1,0:T(8,128)(2,1)} %get-tuple-element.18), calls=%async_computation | async-start | bytes 2949120 | tf_op jit(solution)/shard_map/all_to_all | solution.py:391
  29.4 1.9 collective-permute-start.4
  31.3 3.9 %collective-permute-start.6 = (bf16[4,704,128]{2,1,0:T(8,128)(2,1)}, bf16[4,704,128]{2,1,0:T(8,128)(2,1)}, u32[]{:S(2)}, u32[]{:S(2)}) collective-permute-start(bf16[4,704,128]{2,1,0:T(8,128)(2,1)} %pad_maximum_fusion.refs_2_), channel_id=1, source_target_pairs={{0,56},{8,0},{16,8},{24,16},{32,24},{40,32},{48,40},{56,48},{1,57}... | collective-permute-start | bytes 2162696 | tf_op jit(solution)/shard_map/ppermute | solution.py:385
  35.2 15.3 %collective-permute-done.4.refs_2_ = bf16[4,704,128]{2,1,0:T(8,128)(2,1)} collective-permute-done((bf16[4,704,128]{2,1,0:T(8,128)(2,1)}, bf16[4,704,128]{2,1,0:T(8,128)(2,1)}, u32[]{:S(2)}, u32[]{:S(2)}) %collective-permute-start.4) | collective-permute-done | bytes 720928 | tf_op jit(solution)/shard_map/ppermute | solution.py:385
  50.5 3.2 %collective-permute-start.10 = (bf16[4,704,128]{2,1,0:T(8,128)(2,1)}, bf16[4,704,128]{2,1,0:T(8,128)(2,1)}, u32[]{:S(2)}, u32[]{:S(2)}) collective-permute-start(bf16[4,704,128]{2,1,0:T(8,128)(2,1)} %collective-permute-done.6.refs_4_), channel_id=1, source_target_pairs={{0,56},{8,0},{16,8},{24,16},{32,24},{40,32},{48,40},{56,48},{1,57}... | collective-permute-start | bytes 2162696 | tf_op jit(solution)/shard_map/ppermute | solution.py:385
  53.7 5.7 %collective-permute-done.3 = bf16[4,18,16,576]{3,2,1,0:T(8,128)(2,1)} collective-permute-done((bf16[4,18,16,576]{3,2,1,0:T(8,128)(2,1)}, bf16[4,18,16,576]{3,2,1,0:T(8,128)(2,1)}, u32[]{:S(2)}, u32[]{:S(2)}) %collective-permute-start.3) | collective-permute-done | bytes 1327136 | tf_op jit(solution)/shard_map/ppermute | solution.py:416
  59.5 4.8 %all-to-all-start.1 = ((bf16[4,18,16,576]{3,2,1,0:T(8,128)(2,1)}), bf16[4,18,16,576]{3,2,1,0:T(8,128)(2,1)S(1)}, u32[]{:S(2)}, u32[]{:S(2)}) async-start(bf16[4,18,16,576]{3,2,1,0:T(8,128)(2,1)} %collective-permute-done.3), calls=%async_computation.1 | async-start | bytes 2949120 | tf_op jit(solution)/shard_map/all_to_all | solution.py:391
  64.3 3.8 %collective-permute-done.8.refs_6_ = bf16[4,704,128]{2,1,0:T(8,128)(2,1)} collective-permute-done((bf16[4,704,128]{2,1,0:T(8,128)(2,1)}, bf16[4,704,128]{2,1,0:T(8,128)(2,1)}, u32[]{:S(2)}, u32[]{:S(2)}) %collective-permute-start.8) | collective-permute-done | bytes 720928 | tf_op jit(solution)/shard_map/ppermute | solution.py:385
  68.1 3.2 %collective-permute-start.14 = (bf16[4,704,128]{2,1,0:T(8,128)(2,1)}, bf16[4,704,128]{2,1,0:T(8,128)(2,1)}, u32[]{:S(2)}, u32[]{:S(2)}) collective-permute-start(bf16[4,704,128]{2,1,0:T(8,128)(2,1)} %collective-permute-done.10.refs_8_), channel_id=1, source_target_pairs={{0,56},{8,0},{16,8},{24,16},{32,24},{40,32},{48,40},{56,48},{1,57}... | collective-permute-start | bytes 2162696 | tf_op jit(solution)/shard_map/ppermute | solution.py:385
  72.8 9.1 %all-to-all-done.1.refs_1_ = bf16[4,18,16,576]{3,2,1,0:T(8,128)(2,1)S(1)} async-done(((bf16[4,18,16,576]{3,2,1,0:T(8,128)(2,1)}), bf16[4,18,16,576]{3,2,1,0:T(8,128)(2,1)S(1)}, u32[]{:S(2)}, u32[]{:S(2)}) %all-to-all-start.1) | async-done | bytes 1327136 | tf_op jit(solution)/shard_map/all_to_all | solution.py:391
  82.5 4.8 %collective-permute-done.12.refs_10_ = bf16[4,704,128]{2,1,0:T(8,128)(2,1)} collective-permute-done((bf16[4,704,128]{2,1,0:T(8,128)(2,1)}, bf16[4,704,128]{2,1,0:T(8,128)(2,1)}, u32[]{:S(2)}, u32[]{:S(2)}) %collective-permute-start.12) | collective-permute-done | bytes 720928 | tf_op jit(solution)/shard_map/ppermute | solution.py:385
  90.8 3.2 %collective-permute-start.18 = (bf16[4,704,128]{2,1,0:T(8,128)(2,1)}, bf16[4,704,128]{2,1,0:T(8,128)(2,1)S(1)}, u32[]{:S(2)}, u32[]{:S(2)}) collective-permute-start(bf16[4,704,128]{2,1,0:T(8,128)(2,1)} %collective-permute-done.15.refs_13_), channel_id=1, source_target_pairs={{0,56},{8,0},{16,8},{24,16},{32,24},{40,32},{48,40},{56,48},{1,57}... | collective-permute-start | bytes 2162696 | tf_op jit(solution)/shard_map/ppermute | solution.py:385
  94.1 17.2 %early.1 = (f32[2,12,16,512]{3,2,1,0:T(8,128)}, f32[2,12,16,512]{3,2,1,0:T(8,128)}, f32[2,16,512]{2,1,0:T(8,128)}, bf16[12,128,512]{2,1,0:T(8,128)(2,1)}) custom-call(s32[5]{0:T(128)} %stack.68.info, f32[2,8,128]{2,1,0:T(8,128)} %mul.55.lse_in, bf16[2,512,128]{2,1,0:T(8,128)(2,1)} %bitcast.84, f32[2,4,128]{2,1,0:T(4,128)} %reshape.99.w_in, ...), custom_call_target="tpu_custom_call" | custom-call | flops 16106127360 | bytes 16777216 | tf_op jit(solution)/shard_map/early/pallas_call | solution.py:309
  112.6 21.9 %late.1 = (f32[4,2,136,128]{3,2,1,0:T(8,128)}, bf16[4,1040,128]{2,1,0:T(8,128)(2,1)}, bf16[4,1040,128]{2,1,0:T(8,128)(2,1)}) custom-call(s32[5]{0:T(128)} %stack.68.info, f32[2,8,128]{2,1,0:T(8,128)} %mul.55.lse_in, bf16[2,512,128]{2,1,0:T(8,128)(2,1)} %bitcast.85, f32[2,4,128]{2,1,0:T(4,128)} %reshape.99.w_in, bf16[2,128,512]{2,1,0:T(8,128)(2,1)} %bitcast.94, ...), custom_call_target="tpu_custom_call" | custom-call | flops 11811160064 | bytes 16777216 | tf_op jit(solution)/shard_map/late/pallas_call | solution.py:309
  134.6 4.9 %all-to-all-start.2 = ((f32[4,2,136,128]{3,2,1,0:T(8,128)}), f32[4,2,136,128]{3,2,1,0:T(8,128)S(1)}, u32[]{:S(2)}, u32[]{:S(2)}) async-start(f32[4,2,136,128]{3,2,1,0:T(8,128)} %get-tuple-element.17), calls=%async_computation.2 | async-start | bytes 1114112 | tf_op jit(solution)/shard_map/all_to_all | solution.py:391
  139.6 1.0 fusion.4
  140.5 2.9 %collective-permute-start.21 = (bf16[1040,128]{1,0:T(8,128)(2,1)}, bf16[1040,128]{1,0:T(8,128)(2,1)S(1)}, u32[]{:S(2)}, u32[]{:S(2)}) collective-permute-start(bf16[1040,128]{1,0:T(8,128)(2,1)} %get-tuple-element.22), channel_id=1, source_target_pairs={{0,128},{64,192},{128,0},{192,64},{1,129},{65,193},{129,1},{193,65... | collective-permute-start | bytes 798728 | tf_op jit(solution)/shard_map/ppermute | solution.py:385
  143.8 4.7 %all-to-all-done.2 = f32[4,2,136,128]{3,2,1,0:T(8,128)S(1)} async-done(((f32[4,2,136,128]{3,2,1,0:T(8,128)}), f32[4,2,136,128]{3,2,1,0:T(8,128)S(1)}, u32[]{:S(2)}, u32[]{:S(2)}) %all-to-all-start.2) | async-done | bytes 557088 | tf_op jit(solution)/shard_map/all_to_all | solution.py:391
  149.6 6.2 %collective-permute-done.20 = bf16[1040,128]{1,0:T(8,128)(2,1)S(1)} collective-permute-done((bf16[1040,128]{1,0:T(8,128)(2,1)}, bf16[1040,128]{1,0:T(8,128)(2,1)S(1)}, u32[]{:S(2)}, u32[]{:S(2)}) %collective-permute-start.20) | collective-permute-done | bytes 266272 | tf_op jit(solution)/shard_map/ppermute | solution.py:385
  156.5 1.2 fusion.2
  158.7 18.7 %all-to-all-start.3 = ((bf16[32,48,128]{2,1,0:T(8,128)(2,1)}), bf16[32,48,128]{2,1,0:T(8,128)(2,1)S(1)}, u32[]{:S(2)}, u32[]{:S(2)}) async-start(bf16[32,48,128]{2,1,0:T(8,128)(2,1)} %pad_maximum_fusion.1), calls=%async_computation.3 | async-start | bytes 786432 | tf_op jit(solution)/shard_map/all_to_all | solution.py:480
  177.5 2.2 %collective-permute-start.23 = (f32[4,136,128]{2,1,0:T(8,128)S(1)}, f32[4,136,128]{2,1,0:T(8,128)S(1)}, u32[]{:S(2)}, u32[]{:S(2)}) collective-permute-start(f32[4,136,128]{2,1,0:T(8,128)S(1)} %slice_bitcast_fusion.1), channel_id=1, source_target_pairs={{0,192},{64,128},{128,64},{192,0},{1,193},{65,129},{129,65},{193,1... | collective-permute-start | bytes 835592 | tf_op jit(solution)/shard_map/ppermute | solution.py:416
  179.8 5.6 %collective-permute-done.23 = f32[4,136,128]{2,1,0:T(8,128)S(1)} collective-permute-done((f32[4,136,128]{2,1,0:T(8,128)S(1)}, f32[4,136,128]{2,1,0:T(8,128)S(1)}, u32[]{:S(2)}, u32[]{:S(2)}) %collective-permute-start.23) | collective-permute-done | bytes 278560 | tf_op jit(solution)/shard_map/ppermute | solution.py:416
  187.2 3.0 %all-to-all-done.3 = bf16[32,48,128]{2,1,0:T(8,128)(2,1)S(1)} async-done(((bf16[32,48,128]{2,1,0:T(8,128)(2,1)}), bf16[32,48,128]{2,1,0:T(8,128)(2,1)S(1)}, u32[]{:S(2)}, u32[]{:S(2)}) %all-to-all-start.3) | async-done | bytes 393248 | tf_op jit(solution)/shard_map/all_to_all | solution.py:480
  (106 shorter events, 19.7 us)
Async XLA Ops:
  3.1 13.2 %collective-permute-start = (bf16[704,128]{1,0:T(8,128)(2,1)}, bf16[704,128]{1,0:T(8,128)(2,1)}, u32[]{:S(2)}, u32[]{:S(2)}) collective-permute-start(bf16[704,128]{1,0:T(8,128)(2,1)} %get-tuple-element.27), channel_id=1, source_target_pairs={{0,192},{64,0},{128,64},{192,128},{1,193},{65,1},{129,65},{193,129... | collective-permute-start | bytes 540680 | tf_op jit(solution)/shard_map/ppermute | solution.py:385
  6.1 10.2 %collective-permute-start.1 = (bf16[704,128]{1,0:T(8,128)(2,1)}, bf16[704,128]{1,0:T(8,128)(2,1)}, u32[]{:S(2)}, u32[]{:S(2)}) collective-permute-start(bf16[704,128]{1,0:T(8,128)(2,1)} %get-tuple-element.27), channel_id=1, source_target_pairs={{0,128},{64,192},{128,0},{192,64},{1,129},{65,193},{129,1},{193,65... | collective-permute-start | bytes 540680 | tf_op jit(solution)/shard_map/ppermute | solution.py:385
  6.8 11.1 %collective-permute-start.2 = (bf16[704,128]{1,0:T(8,128)(2,1)}, bf16[704,128]{1,0:T(8,128)(2,1)}, u32[]{:S(2)}, u32[]{:S(2)}) collective-permute-start(bf16[704,128]{1,0:T(8,128)(2,1)} %get-tuple-element.27), channel_id=1, source_target_pairs={{0,64},{64,128},{128,192},{192,0},{1,65},{65,129},{129,193},{193,1... | collective-permute-start | bytes 540680 | tf_op jit(solution)/shard_map/ppermute | solution.py:385
  23.7 35.7 %collective-permute-start.3 = (bf16[4,18,16,576]{3,2,1,0:T(8,128)(2,1)}, bf16[4,18,16,576]{3,2,1,0:T(8,128)(2,1)}, u32[]{:S(2)}, u32[]{:S(2)}) collective-permute-start(bf16[4,18,16,576]{3,2,1,0:T(8,128)(2,1)} %get-tuple-element.19), channel_id=1, source_target_pairs={{0,192},{64,128},{128,64},{192,0},{1,193},{65,129},{129,65},{193,1... | collective-permute-start | bytes 3981320 | tf_op jit(solution)/shard_map/ppermute | solution.py:416
  24.5 29.2 %all-to-all-start = ((bf16[4,18,16,576]{3,2,1,0:T(8,128)(2,1)}), bf16[4,18,16,576]{3,2,1,0:T(8,128)(2,1)S(1)}, u32[]{:S(2)}, u32[]{:S(2)}) async-start(bf16[4,18,16,576]{3,2,1,0:T(8,128)(2,1)} %get-tuple-element.18), calls=%async_computation | async-start | bytes 2949120 | tf_op jit(solution)/shard_map/all_to_all | solution.py:391
  29.4 21.1 %collective-permute-start.4 = (bf16[4,704,128]{2,1,0:T(8,128)(2,1)}, bf16[4,704,128]{2,1,0:T(8,128)(2,1)}, u32[]{:S(2)}, u32[]{:S(2)}) collective-permute-start(bf16[4,704,128]{2,1,0:T(8,128)(2,1)} %pad_maximum_fusion.refs_2_), channel_id=1, source_target_pairs={{0,8},{8,16},{16,24},{24,32},{32,40},{40,48},{48,56},{56,0},{1,9},... | collective-permute-start | bytes 2162696 | tf_op jit(solution)/shard_map/ppermute | solution.py:385
  31.3 19.2 %collective-permute-start.6 = (bf16[4,704,128]{2,1,0:T(8,128)(2,1)}, bf16[4,704,128]{2,1,0:T(8,128)(2,1)}, u32[]{:S(2)}, u32[]{:S(2)}) collective-permute-start(bf16[4,704,128]{2,1,0:T(8,128)(2,1)} %pad_maximum_fusion.refs_2_), channel_id=1, source_target_pairs={{0,56},{8,0},{16,8},{24,16},{32,24},{40,32},{48,40},{56,48},{1,57}... | collective-permute-start | bytes 2162696 | tf_op jit(solution)/shard_map/ppermute | solution.py:385
  50.5 17.6 %collective-permute-start.8 = (bf16[4,704,128]{2,1,0:T(8,128)(2,1)}, bf16[4,704,128]{2,1,0:T(8,128)(2,1)}, u32[]{:S(2)}, u32[]{:S(2)}) collective-permute-start(bf16[4,704,128]{2,1,0:T(8,128)(2,1)} %collective-permute-done.4.refs_2_), channel_id=1, source_target_pairs={{0,8},{8,16},{16,24},{24,32},{32,40},{40,48},{48,56},{56,0},{1,9},... | collective-permute-start | bytes 2162696 | tf_op jit(solution)/shard_map/ppermute | solution.py:385
  50.5 17.6 %collective-permute-start.10 = (bf16[4,704,128]{2,1,0:T(8,128)(2,1)}, bf16[4,704,128]{2,1,0:T(8,128)(2,1)}, u32[]{:S(2)}, u32[]{:S(2)}) collective-permute-start(bf16[4,704,128]{2,1,0:T(8,128)(2,1)} %collective-permute-done.6.refs_4_), channel_id=1, source_target_pairs={{0,56},{8,0},{16,8},{24,16},{32,24},{40,32},{48,40},{56,48},{1,57}... | collective-permute-start | bytes 2162696 | tf_op jit(solution)/shard_map/ppermute | solution.py:385
  53.7 18.2 %copy-start = (bf16[4,18,16,576]{3,2,1,0:T(8,128)(2,1)}, bf16[4,18,16,576]{3,2,1,0:T(8,128)(2,1)S(1)}, u32[]{:S(2)}) copy-start(bf16[4,18,16,576]{3,2,1,0:T(8,128)(2,1)S(1)} %all-to-all-done.refs_0_) | copy-start | bytes 3981316
  59.5 22.4 %all-to-all-start.1 = ((bf16[4,18,16,576]{3,2,1,0:T(8,128)(2,1)}), bf16[4,18,16,576]{3,2,1,0:T(8,128)(2,1)S(1)}, u32[]{:S(2)}, u32[]{:S(2)}) async-start(bf16[4,18,16,576]{3,2,1,0:T(8,128)(2,1)} %collective-permute-done.3), calls=%async_computation.1 | async-start | bytes 2949120 | tf_op jit(solution)/shard_map/all_to_all | solution.py:391
  64.3 18.1 %collective-permute-start.5 = (bf16[4,704,128]{2,1,0:T(8,128)(2,1)}, bf16[4,704,128]{2,1,0:T(8,128)(2,1)}, u32[]{:S(2)}, u32[]{:S(2)}) collective-permute-start(bf16[4,704,128]{2,1,0:T(8,128)(2,1)} %collective-permute-done.4.refs_2_), channel_id=1, source_target_pairs={{0,4},{4,0},{1,5},{5,1},{2,6},{6,2},{3,7},{7,3},{8,12},{12,8},{9,1... | collective-permute-start | bytes 2162696 | tf_op jit(solution)/shard_map/ppermute | solution.py:385
  68.1 19.2 %collective-permute-start.12 = (bf16[4,704,128]{2,1,0:T(8,128)(2,1)}, bf16[4,704,128]{2,1,0:T(8,128)(2,1)}, u32[]{:S(2)}, u32[]{:S(2)}) collective-permute-start(bf16[4,704,128]{2,1,0:T(8,128)(2,1)} %collective-permute-done.8.refs_6_), channel_id=1, source_target_pairs={{0,8},{8,16},{16,24},{24,32},{32,40},{40,48},{48,56},{56,0},{1,9},... | collective-permute-start | bytes 2162696 | tf_op jit(solution)/shard_map/ppermute | solution.py:385
  68.1 19.2 %collective-permute-start.14 = (bf16[4,704,128]{2,1,0:T(8,128)(2,1)}, bf16[4,704,128]{2,1,0:T(8,128)(2,1)}, u32[]{:S(2)}, u32[]{:S(2)}) collective-permute-start(bf16[4,704,128]{2,1,0:T(8,128)(2,1)} %collective-permute-done.10.refs_8_), channel_id=1, source_target_pairs={{0,56},{8,0},{16,8},{24,16},{32,24},{40,32},{48,40},{56,48},{1,57}... | collective-permute-start | bytes 2162696 | tf_op jit(solution)/shard_map/ppermute | solution.py:385
  72.0 18.8 %collective-permute-start.7 = (bf16[4,704,128]{2,1,0:T(8,128)(2,1)}, bf16[4,704,128]{2,1,0:T(8,128)(2,1)}, u32[]{:S(2)}, u32[]{:S(2)}) collective-permute-start(bf16[4,704,128]{2,1,0:T(8,128)(2,1)} %collective-permute-done.6.refs_4_), channel_id=1, source_target_pairs={{0,4},{4,0},{1,5},{5,1},{2,6},{6,2},{3,7},{7,3},{8,12},{12,8},{9,1... | collective-permute-start | bytes 2162696 | tf_op jit(solution)/shard_map/ppermute | solution.py:385
  72.0 18.8 %collective-permute-start.11 = (bf16[4,704,128]{2,1,0:T(8,128)(2,1)}, bf16[4,704,128]{2,1,0:T(8,128)(2,1)}, u32[]{:S(2)}, u32[]{:S(2)}) collective-permute-start(bf16[4,704,128]{2,1,0:T(8,128)(2,1)} %collective-permute-done.10.refs_8_), channel_id=1, source_target_pairs={{0,4},{4,0},{1,5},{5,1},{2,6},{6,2},{3,7},{7,3},{8,12},{12,8},{9,1... | collective-permute-start | bytes 2162696 | tf_op jit(solution)/shard_map/ppermute | solution.py:385
  81.8 6.1 %copy-start.1 = (bf16[4,18,16,576]{3,2,1,0:T(8,128)(2,1)}, bf16[4,18,16,576]{3,2,1,0:T(8,128)(2,1)S(1)}, u32[]{:S(2)}) copy-start(bf16[4,18,16,576]{3,2,1,0:T(8,128)(2,1)S(1)} %all-to-all-done.1.refs_1_) | copy-start | bytes 3981316
  82.4 11.6 %collective-permute-start.9 = (bf16[4,704,128]{2,1,0:T(8,128)(2,1)}, bf16[4,704,128]{2,1,0:T(8,128)(2,1)}, u32[]{:S(2)}, u32[]{:S(2)}) collective-permute-start(bf16[4,704,128]{2,1,0:T(8,128)(2,1)} %collective-permute-done.8.refs_6_), channel_id=1, source_target_pairs={{0,4},{4,0},{1,5},{5,1},{2,6},{6,2},{3,7},{7,3},{8,12},{12,8},{9,1... | collective-permute-start | bytes 2162696 | tf_op jit(solution)/shard_map/ppermute | solution.py:385
  87.3 6.8 %collective-permute-start.13 = (bf16[4,704,128]{2,1,0:T(8,128)(2,1)}, bf16[4,704,128]{2,1,0:T(8,128)(2,1)}, u32[]{:S(2)}, u32[]{:S(2)}) collective-permute-start(bf16[4,704,128]{2,1,0:T(8,128)(2,1)} %collective-permute-done.12.refs_10_), channel_id=1, source_target_pairs={{0,4},{4,0},{1,5},{5,1},{2,6},{6,2},{3,7},{7,3},{8,12},{12,8},{9,1... | collective-permute-start | bytes 2162696 | tf_op jit(solution)/shard_map/ppermute | solution.py:385
  87.3 3.6 %collective-permute-start.15 = (bf16[4,704,128]{2,1,0:T(8,128)(2,1)}, bf16[4,704,128]{2,1,0:T(8,128)(2,1)}, u32[]{:S(2)}, u32[]{:S(2)}) collective-permute-start(bf16[4,704,128]{2,1,0:T(8,128)(2,1)} %collective-permute-done.14.refs_12_), channel_id=1, source_target_pairs={{0,4},{4,0},{1,5},{5,1},{2,6},{6,2},{3,7},{7,3},{8,12},{12,8},{9,1... | collective-permute-start | bytes 2162696 | tf_op jit(solution)/shard_map/ppermute | solution.py:385
  87.9 6.1 %copy-start.3 = (bf16[2,4,8,16,128]{4,3,2,1,0:T(8,128)(2,1)}, bf16[2,4,8,16,128]{4,3,2,1,0:T(8,128)(2,1)S(1)}, u32[]{:S(2)}) copy-start(bf16[2,4,8,16,128]{4,3,2,1,0:T(8,128)(2,1)S(1)} %copy.33) | copy-start | bytes 786436
  90.7 20.6 %collective-permute-start.16 = (bf16[4,704,128]{2,1,0:T(8,128)(2,1)}, bf16[4,704,128]{2,1,0:T(8,128)(2,1)S(1)}, u32[]{:S(2)}, u32[]{:S(2)}) collective-permute-start(bf16[4,704,128]{2,1,0:T(8,128)(2,1)} %pad_maximum_fusion.refs_2_), channel_id=1, source_target_pairs={{0,4},{4,0},{1,5},{5,1},{2,6},{6,2},{3,7},{7,3},{8,12},{12,8},{9,1... | collective-permute-start | bytes 2162696 | tf_op jit(solution)/shard_map/ppermute | solution.py:385
  90.7 20.6 %collective-permute-start.17 = (bf16[4,704,128]{2,1,0:T(8,128)(2,1)}, bf16[4,704,128]{2,1,0:T(8,128)(2,1)S(1)}, u32[]{:S(2)}, u32[]{:S(2)}) collective-permute-start(bf16[4,704,128]{2,1,0:T(8,128)(2,1)} %collective-permute-done.12.refs_10_), channel_id=1, source_target_pairs={{0,8},{8,16},{16,24},{24,32},{32,40},{40,48},{48,56},{56,0},{1,9},... | collective-permute-start | bytes 2162696 | tf_op jit(solution)/shard_map/ppermute | solution.py:385
  90.8 20.5 %collective-permute-start.18 = (bf16[4,704,128]{2,1,0:T(8,128)(2,1)}, bf16[4,704,128]{2,1,0:T(8,128)(2,1)S(1)}, u32[]{:S(2)}, u32[]{:S(2)}) collective-permute-start(bf16[4,704,128]{2,1,0:T(8,128)(2,1)} %collective-permute-done.15.refs_13_), channel_id=1, source_target_pairs={{0,56},{8,0},{16,8},{24,16},{32,24},{40,32},{48,40},{56,48},{1,57}... | collective-permute-start | bytes 2162696 | tf_op jit(solution)/shard_map/ppermute | solution.py:385
  134.5 5.1 %copy-start.2 = (bf16[4,1040,128]{2,1,0:T(8,128)(2,1)S(1)}, bf16[4,1040,128]{2,1,0:T(8,128)(2,1)}, u32[]{:S(2)}) copy-start(bf16[4,1040,128]{2,1,0:T(8,128)(2,1)} %get-tuple-element.15) | copy-start | bytes 3194884
  134.5 5.0 %collective-permute-start.19 = (bf16[4,1040,128]{2,1,0:T(8,128)(2,1)}, bf16[4,1040,128]{2,1,0:T(8,128)(2,1)S(1)}, u32[]{:S(2)}, u32[]{:S(2)}) collective-permute-start(bf16[4,1040,128]{2,1,0:T(8,128)(2,1)} %get-tuple-element.16), channel_id=1, source_target_pairs={{0,4},{4,0},{1,5},{5,1},{2,6},{6,2},{3,7},{7,3},{8,12},{12,8},{9,1... | collective-permute-start | bytes 3194888 | tf_op jit(solution)/shard_map/ppermute | solution.py:385
  134.6 13.8 %all-to-all-start.2 = ((f32[4,2,136,128]{3,2,1,0:T(8,128)}), f32[4,2,136,128]{3,2,1,0:T(8,128)S(1)}, u32[]{:S(2)}, u32[]{:S(2)}) async-start(f32[4,2,136,128]{3,2,1,0:T(8,128)} %get-tuple-element.17), calls=%async_computation.2 | async-start | bytes 1114112 | tf_op jit(solution)/shard_map/all_to_all | solution.py:391
  140.5 15.2 %collective-permute-start.20 = (bf16[1040,128]{1,0:T(8,128)(2,1)}, bf16[1040,128]{1,0:T(8,128)(2,1)S(1)}, u32[]{:S(2)}, u32[]{:S(2)}) collective-permute-start(bf16[1040,128]{1,0:T(8,128)(2,1)} %get-tuple-element.20), channel_id=1, source_target_pairs={{0,64},{64,128},{128,192},{192,0},{1,65},{65,129},{129,193},{193,1... | collective-permute-start | bytes 798728 | tf_op jit(solution)/shard_map/ppermute | solution.py:385
  140.5 15.2 %collective-permute-start.21 = (bf16[1040,128]{1,0:T(8,128)(2,1)}, bf16[1040,128]{1,0:T(8,128)(2,1)S(1)}, u32[]{:S(2)}, u32[]{:S(2)}) collective-permute-start(bf16[1040,128]{1,0:T(8,128)(2,1)} %get-tuple-element.22), channel_id=1, source_target_pairs={{0,128},{64,192},{128,0},{192,64},{1,129},{65,193},{129,1},{193,65... | collective-permute-start | bytes 798728 | tf_op jit(solution)/shard_map/ppermute | solution.py:385
  143.5 13.0 %collective-permute-start.22 = (bf16[1040,128]{1,0:T(8,128)(2,1)S(1)}, bf16[1040,128]{1,0:T(8,128)(2,1)}, u32[]{:S(2)}, u32[]{:S(2)}) collective-permute-start(bf16[1040,128]{1,0:T(8,128)(2,1)S(1)} %get-tuple-element.21), channel_id=1, source_target_pairs={{0,192},{64,0},{128,64},{192,128},{1,193},{65,1},{129,65},{193,129... | collective-permute-start | bytes 798728 | tf_op jit(solution)/shard_map/ppermute | solution.py:385
  158.7 31.5 %all-to-all-start.3 = ((bf16[32,48,128]{2,1,0:T(8,128)(2,1)}), bf16[32,48,128]{2,1,0:T(8,128)(2,1)S(1)}, u32[]{:S(2)}, u32[]{:S(2)}) async-start(bf16[32,48,128]{2,1,0:T(8,128)(2,1)} %pad_maximum_fusion.1), calls=%async_computation.3 | async-start | bytes 786432 | tf_op jit(solution)/shard_map/all_to_all | solution.py:480
  177.5 7.9 %collective-permute-start.23 = (f32[4,136,128]{2,1,0:T(8,128)S(1)}, f32[4,136,128]{2,1,0:T(8,128)S(1)}, u32[]{:S(2)}, u32[]{:S(2)}) collective-permute-start(f32[4,136,128]{2,1,0:T(8,128)S(1)} %slice_bitcast_fusion.1), channel_id=1, source_target_pairs={{0,192},{64,128},{128,64},{192,0},{1,193},{65,129},{129,65},{193,1... | collective-permute-start | bytes 835592 | tf_op jit(solution)/shard_map/ppermute | solution.py:416
  (4 other events, 4.1 us)
